TPU v7x, 512 devices: a whole 4x4x16 slice. The times are simulated.
512 devices in a mesh: chain: 64 (over z, y), rows: 8 (over x, core).
Axes of the slice: x: 4, y: 4, z: 16, core: 2. Of those that a mesh axis runs over, the one named last changes fastest.
Arguments:
- rhs: float32 [512, 32768], P('rows', 'chain'), may hold values from -3 to 3
- diag_factors: float32 [9, 512, 512], P(None, 'rows'), may hold values from -1 to 1
- left_factors: float32 [9, 512, 512], P(None, 'rows'), may hold values from -0.1875 to 0.1875
- right_factors: float32 [9, 512, 512], P(None, 'rows'), may hold values from -0.1875 to 0.1875
Outputs:
- voltages: float32 [512, 32768], P('rows', 'chain')
All inputs are finite; a program needn't handle non-finite values.
Results may differ from a plain program's by a relative error of at most 0.00019.
Values sent between devices are 32-bit elements; how exact they have to be, the bound alone decides.
A program may use at most 64 MiB of HBM per device.

v0:
```python
import jax
import jax.numpy as jnp
from jax import lax
from jax.sharding import PartitionSpec as P

NRHS = 64


def from_behind(value, axis, steps):
    count = lax.axis_size(axis)
    first, last = (max(0, -steps), min(count, count - steps))
    return lax.ppermute(value, axis, [(source, source + steps) for source in range(first, last)])


def level_products(stacked, current, level):
    window = stacked[level]
    return jnp.dot(
        window,
        lax.all_gather(current, "rows", axis=0, tiled=True),
        precision=lax.Precision.HIGHEST,
        preferred_element_type=jnp.float32,
    )


def on_device(rhs, diag_factors, left_factors, right_factors):
    rows_dev = rhs.shape[0]
    levels = diag_factors.shape[0]
    blocks = rhs.shape[1] // NRHS
    stacked = jnp.concatenate((diag_factors, left_factors, right_factors), axis=1)
    columns = blocks * NRHS
    current = rhs
    for level in range(levels):
        distance = 2**level
        edge_cols = min(distance, blocks) * NRHS
        device_hop = max(1, distance // blocks)
        products = level_products(stacked, current, level)
        own_term = products[:rows_dev]
        left_flat = products[rows_dev : 2 * rows_dev]
        right_flat = products[2 * rows_dev :]
        arrived_left = from_behind(left_flat[:, columns - edge_cols :], "chain", device_hop)
        arrived_right = from_behind(right_flat[:, :edge_cols], "chain", -device_hop)
        left_in = jnp.concatenate((arrived_left, left_flat[:, : columns - edge_cols]), axis=1)
        right_in = jnp.concatenate((right_flat[:, edge_cols:], arrived_right), axis=1)
        current = own_term - left_in - right_in
    return current


def solution(mesh):
    placed = (
        P("rows", "chain"),
        P(None, "rows", None),
        P(None, "rows", None),
        P(None, "rows", None),
    )
    return jax.shard_map(
        on_device, mesh=mesh, in_specs=placed, out_specs=P("rows", "chain"), check_vma=False
    )
```

profile of v0, /device:TPU:1, one launch (start us, length us, event | category | flops | bytes accessed | tf_op | source)
XLA Modules:
  0.0 466.1 jit_solution(8815618490947886444)
XLA Ops:
  7.3 1.4 constant_dynamic-update-slice_fusion.2
  8.8 1.4 constant_dynamic-update-slice_fusion.1
  10.2 36.2 %all-gather.10.cloned.1.call-done = f32[512,512]{1,0:T(8,128)} async-done(((f32[64,512]{1,0:T(8,128)}), f32[512,512]{1,0:T(8,128)}) %all-gather.10.cloned.1.call-update) | async-done | bytes 1048592 | tf_op jit(solution)/shard_map/all_gather | solution.py:19
  46.4 2.1 fusion
  48.6 2.9 collective-permute-start
  51.6 1.3 collective-permute-start.1
  53.0 3.2 collective-permute-done.1
  57.1 34.7 %all-gather.12.cloned.1.call-done = f32[512,512]{1,0:T(8,128)} async-done(((f32[64,512]{1,0:T(8,128)}), f32[512,512]{1,0:T(8,128)}) %all-gather.12.cloned.1.call-update) | async-done | bytes 1048592 | tf_op jit(solution)/shard_map/all_gather | solution.py:19
  91.8 2.1 fusion.1
  93.9 2.9 collective-permute-start.2
  98.2 3.3 collective-permute-done.3
  102.3 34.7 %all-gather.14.cloned.1.call-done = f32[512,512]{1,0:T(8,128)} async-done(((f32[64,512]{1,0:T(8,128)}), f32[512,512]{1,0:T(8,128)}) %all-gather.14.cloned.1.call-update) | async-done | bytes 1048592 | tf_op jit(solution)/shard_map/all_gather | solution.py:19
  137.0 2.1 fusion.2
  139.1 2.9 collective-permute-start.4
  143.4 3.7 collective-permute-done.5
  147.9 34.7 %all-gather.16.cloned.1.call-done = f32[512,512]{1,0:T(8,128)} async-done(((f32[64,512]{1,0:T(8,128)}), f32[512,512]{1,0:T(8,128)}) %all-gather.16.cloned.1.call-update) | async-done | bytes 1048592 | tf_op jit(solution)/shard_map/all_gather | solution.py:19
  182.6 2.1 fusion.3
  184.7 2.9 collective-permute-start.6
  187.7 1.3 collective-permute-start.7
  189.0 1.3 collective-permute-done.6
  190.3 3.8 collective-permute-done.7
  194.8 34.4 %all-gather.18.cloned.1.call-done = f32[512,512]{1,0:T(8,128)} async-done(((f32[64,512]{1,0:T(8,128)}), f32[512,512]{1,0:T(8,128)}) %all-gather.18.cloned.1.call-update) | async-done | bytes 1048592 | tf_op jit(solution)/shard_map/all_gather | solution.py:19
  229.2 2.1 fusion.4
  231.4 4.5 collective-permute-start.8
  237.2 1.3 collective-permute-done.8
  238.5 5.3 %collective-permute-done.9 = f32[64,512]{1,0:T(8,128)S(1)} collective-permute-done((f32[64,512]{1,0:T(8,128)S(1)}, f32[64,512]{1,0:T(8,128)S(1)}, u32[]{:S(2)}, u32[]{:S(2)}) %collective-permute-start.9) | collective-permute-done | bytes 131104 | tf_op jit(solution)/shard_map/ppermute | solution.py:12
  244.5 32.6 %all-gather.20.cloned.1.call-done = f32[512,512]{1,0:T(8,128)} async-done(((f32[64,512]{1,0:T(8,128)}), f32[512,512]{1,0:T(8,128)}) %all-gather.20.cloned.1.call-update) | async-done | bytes 1048592 | tf_op jit(solution)/shard_map/all_gather | solution.py:19
  277.1 2.1 fusion.5
  279.2 3.0 collective-permute-start.10
  282.3 1.3 collective-permute-start.11
  283.6 1.3 collective-permute-done.10
  284.9 3.8 collective-permute-done.11
  289.5 32.6 %all-gather.22.cloned.1.call-done = f32[512,512]{1,0:T(8,128)} async-done(((f32[64,512]{1,0:T(8,128)}), f32[512,512]{1,0:T(8,128)}) %all-gather.22.cloned.1.call-update) | async-done | bytes 1048592 | tf_op jit(solution)/shard_map/all_gather | solution.py:19
  322.0 2.1 fusion.6
  324.1 4.0 collective-permute-start.12
  328.2 1.3 collective-permute-start.13
  329.5 1.4 collective-permute-done.12
  330.9 8.4 %collective-permute-done.13 = f32[64,512]{1,0:T(8,128)S(1)} collective-permute-done((f32[64,512]{1,0:T(8,128)S(1)}, f32[64,512]{1,0:T(8,128)S(1)}, u32[]{:S(2)}, u32[]{:S(2)}) %collective-permute-start.13) | collective-permute-done | bytes 131104 | tf_op jit(solution)/shard_map/ppermute | solution.py:12
  340.0 30.6 %all-gather.24.cloned.1.call-done = f32[512,512]{1,0:T(8,128)} async-done(((f32[64,512]{1,0:T(8,128)}), f32[512,512]{1,0:T(8,128)}) %all-gather.24.cloned.1.call-update) | async-done | bytes 1048592 | tf_op jit(solution)/shard_map/all_gather | solution.py:19
  370.6 2.1 fusion.7
  372.7 7.2 %collective-permute-start.14 = (f32[64,512]{1,0:T(8,128)S(1)}, f32[64,512]{1,0:T(8,128)S(1)}, u32[]{:S(2)}, u32[]{:S(2)}) collective-permute-start(f32[64,512]{1,0:T(8,128)S(1)} %get-tuple-element.7), channel_id=1, source_target_pairs={{0,128},{8,136},{16,144},{24,152},{32,160},{40,168},{48,176},{56,1... | collective-permute-start | bytes 393224 | tf_op jit(solution)/shard_map/ppermute | solution.py:12
  381.2 1.4 collective-permute-done.14
  382.6 16.3 %collective-permute-done.15 = f32[64,512]{1,0:T(8,128)S(1)} collective-permute-done((f32[64,512]{1,0:T(8,128)S(1)}, f32[64,512]{1,0:T(8,128)S(1)}, u32[]{:S(2)}, u32[]{:S(2)}) %collective-permute-start.15) | collective-permute-done | bytes 131104 | tf_op jit(solution)/shard_map/ppermute | solution.py:12
  399.6 27.4 %all-gather.26.cloned.1.call-done = f32[512,512]{1,0:T(8,128)} async-done(((f32[64,512]{1,0:T(8,128)}), f32[512,512]{1,0:T(8,128)}) %all-gather.26.cloned.1.call-update) | async-done | bytes 1048592 | tf_op jit(solution)/shard_map/all_gather | solution.py:19
  427.0 2.1 fusion.8
  429.1 12.4 %collective-permute-start.16 = (f32[64,512]{1,0:T(8,128)S(1)}, f32[64,512]{1,0:T(8,128)S(1)}, u32[]{:S(2)}, u32[]{:S(2)}) collective-permute-start(f32[64,512]{1,0:T(8,128)S(1)} %get-tuple-element.5), channel_id=1, source_target_pairs={{0,256},{8,264},{16,272},{24,280},{32,288},{40,296},{48,304},{56,3... | collective-permute-start | bytes 393224 | tf_op jit(solution)/shard_map/ppermute | solution.py:12
  442.8 1.3 collective-permute-done.16
  444.1 14.8 %collective-permute-done.17 = f32[64,512]{1,0:T(8,128)S(1)} collective-permute-done((f32[64,512]{1,0:T(8,128)S(1)}, f32[64,512]{1,0:T(8,128)S(1)}, u32[]{:S(2)}, u32[]{:S(2)}) %collective-permute-start.17) | collective-permute-done | bytes 131104 | tf_op jit(solution)/shard_map/ppermute | solution.py:12
  (49 shorter events, 14.3 us)
Async XLA Ops:
  6.5 39.9 %all-gather.10.cloned.1.call-start = ((), (), s32[]{:S(2)}) async-start(), calls=%async_computation | async-start | bytes 1179648 | tf_op jit(solution)/shard_map/all_gather | solution.py:19
  7.3 84.5 %all-gather.12.cloned.1.call-start = ((), (), s32[]{:S(2)}) async-start(), calls=%async_computation.1 | async-start | bytes 1179648 | tf_op jit(solution)/shard_map/all_gather | solution.py:19
  7.3 2.8 copy-start
  48.6 4.3 collective-permute-start
  51.6 4.7 collective-permute-start.1
  57.0 80.0 %all-gather.14.cloned.1.call-start = ((), (), s32[]{:S(2)}) async-start(), calls=%async_computation.2 | async-start | bytes 1179648 | tf_op jit(solution)/shard_map/all_gather | solution.py:19
  93.9 4.3 collective-permute-start.2
  96.9 4.7 collective-permute-start.3
  102.2 80.4 %all-gather.16.cloned.1.call-start = ((), (), s32[]{:S(2)}) async-start(), calls=%async_computation.3 | async-start | bytes 1179648 | tf_op jit(solution)/shard_map/all_gather | solution.py:19
  139.1 4.3 collective-permute-start.4
  142.1 5.0 %collective-permute-start.5 = (f32[64,256]{1,0:T(8,128)S(1)}, f32[64,256]{1,0:T(8,128)S(1)}, u32[]{:S(2)}, u32[]{:S(2)}) collective-permute-start(f32[64,256]{1,0:T(8,128)S(1)} %get-tuple-element.18), channel_id=1, source_target_pairs={{8,0},{16,8},{24,16},{32,24},{40,32},{48,40},{56,48},{64,56},{72,6... | collective-permute-start | bytes 196616 | tf_op jit(solution)/shard_map/ppermute | solution.py:12
  147.8 81.4 %all-gather.18.cloned.1.call-start = ((), (), s32[]{:S(2)}) async-start(), calls=%async_computation.4 | async-start | bytes 1179648 | tf_op jit(solution)/shard_map/all_gather | solution.py:19
  184.7 5.6 %collective-permute-start.6 = (f32[64,512]{1,0:T(8,128)S(1)}, f32[64,512]{1,0:T(8,128)S(1)}, u32[]{:S(2)}, u32[]{:S(2)}) collective-permute-start(f32[64,512]{1,0:T(8,128)S(1)} %get-tuple-element.15), channel_id=1, source_target_pairs={{0,8},{8,16},{16,24},{24,32},{32,40},{40,48},{48,56},{56,64},{64,7... | collective-permute-start | bytes 393224 | tf_op jit(solution)/shard_map/ppermute | solution.py:12
  187.7 6.4 %collective-permute-start.7 = (f32[64,512]{1,0:T(8,128)S(1)}, f32[64,512]{1,0:T(8,128)S(1)}, u32[]{:S(2)}, u32[]{:S(2)}) collective-permute-start(f32[64,512]{1,0:T(8,128)S(1)} %get-tuple-element.16), channel_id=1, source_target_pairs={{8,0},{16,8},{24,16},{32,24},{40,32},{48,40},{56,48},{64,56},{72,6... | collective-permute-start | bytes 393224 | tf_op jit(solution)/shard_map/ppermute | solution.py:12
  194.8 82.3 %all-gather.20.cloned.1.call-start = ((), (), s32[]{:S(2)}) async-start(), calls=%async_computation.5 | async-start | bytes 1179648 | tf_op jit(solution)/shard_map/all_gather | solution.py:19
  231.4 7.1 %collective-permute-start.8 = (f32[64,512]{1,0:T(8,128)S(1)}, f32[64,512]{1,0:T(8,128)S(1)}, u32[]{:S(2)}, u32[]{:S(2)}) collective-permute-start(f32[64,512]{1,0:T(8,128)S(1)} %get-tuple-element.13), channel_id=1, source_target_pairs={{0,16},{8,24},{16,32},{24,40},{32,48},{40,56},{48,64},{56,72},{64,... | collective-permute-start | bytes 393224 | tf_op jit(solution)/shard_map/ppermute | solution.py:12
  235.8 7.9 %collective-permute-start.9 = (f32[64,512]{1,0:T(8,128)S(1)}, f32[64,512]{1,0:T(8,128)S(1)}, u32[]{:S(2)}, u32[]{:S(2)}) collective-permute-start(f32[64,512]{1,0:T(8,128)S(1)} %get-tuple-element.14), channel_id=1, source_target_pairs={{16,0},{24,8},{32,16},{40,24},{48,32},{56,40},{64,48},{72,56},{80,... | collective-permute-start | bytes 393224 | tf_op jit(solution)/shard_map/ppermute | solution.py:12
  244.5 77.5 %all-gather.22.cloned.1.call-start = ((), (), s32[]{:S(2)}) async-start(), calls=%async_computation.6 | async-start | bytes 1179648 | tf_op jit(solution)/shard_map/all_gather | solution.py:19
  279.2 5.7 %collective-permute-start.10 = (f32[64,512]{1,0:T(8,128)S(1)}, f32[64,512]{1,0:T(8,128)S(1)}, u32[]{:S(2)}, u32[]{:S(2)}) collective-permute-start(f32[64,512]{1,0:T(8,128)S(1)} %get-tuple-element.11), channel_id=1, source_target_pairs={{0,32},{8,40},{16,48},{24,56},{32,64},{40,72},{48,80},{56,88},{64,... | collective-permute-start | bytes 393224 | tf_op jit(solution)/shard_map/ppermute | solution.py:12
  282.3 6.4 %collective-permute-start.11 = (f32[64,512]{1,0:T(8,128)S(1)}, f32[64,512]{1,0:T(8,128)S(1)}, u32[]{:S(2)}, u32[]{:S(2)}) collective-permute-start(f32[64,512]{1,0:T(8,128)S(1)} %get-tuple-element.12), channel_id=1, source_target_pairs={{32,0},{40,8},{48,16},{56,24},{64,32},{72,40},{80,48},{88,56},{96,... | collective-permute-start | bytes 393224 | tf_op jit(solution)/shard_map/ppermute | solution.py:12
  289.4 81.2 %all-gather.24.cloned.1.call-start = ((), (), s32[]{:S(2)}) async-start(), calls=%async_computation.7 | async-start | bytes 1179648 | tf_op jit(solution)/shard_map/all_gather | solution.py:19
  324.1 6.7 %collective-permute-start.12 = (f32[64,512]{1,0:T(8,128)S(1)}, f32[64,512]{1,0:T(8,128)S(1)}, u32[]{:S(2)}, u32[]{:S(2)}) collective-permute-start(f32[64,512]{1,0:T(8,128)S(1)} %get-tuple-element.9), channel_id=1, source_target_pairs={{0,64},{8,72},{16,80},{24,88},{32,96},{40,104},{48,112},{56,120},{... | collective-permute-start | bytes 393224 | tf_op jit(solution)/shard_map/ppermute | solution.py:12
  328.2 11.1 %collective-permute-start.13 = (f32[64,512]{1,0:T(8,128)S(1)}, f32[64,512]{1,0:T(8,128)S(1)}, u32[]{:S(2)}, u32[]{:S(2)}) collective-permute-start(f32[64,512]{1,0:T(8,128)S(1)} %get-tuple-element.10), channel_id=1, source_target_pairs={{64,0},{72,8},{80,16},{88,24},{96,32},{104,40},{112,48},{120,56},{... | collective-permute-start | bytes 393224 | tf_op jit(solution)/shard_map/ppermute | solution.py:12
  340.0 87.0 %all-gather.26.cloned.1.call-start = ((), (), s32[]{:S(2)}) async-start(), calls=%async_computation.8 | async-start | bytes 1179648 | tf_op jit(solution)/shard_map/all_gather | solution.py:19
  372.7 9.9 %collective-permute-start.14 = (f32[64,512]{1,0:T(8,128)S(1)}, f32[64,512]{1,0:T(8,128)S(1)}, u32[]{:S(2)}, u32[]{:S(2)}) collective-permute-start(f32[64,512]{1,0:T(8,128)S(1)} %get-tuple-element.7), channel_id=1, source_target_pairs={{0,128},{8,136},{16,144},{24,152},{32,160},{40,168},{48,176},{56,1... | collective-permute-start | bytes 393224 | tf_op jit(solution)/shard_map/ppermute | solution.py:12
  379.9 19.0 %collective-permute-start.15 = (f32[64,512]{1,0:T(8,128)S(1)}, f32[64,512]{1,0:T(8,128)S(1)}, u32[]{:S(2)}, u32[]{:S(2)}) collective-permute-start(f32[64,512]{1,0:T(8,128)S(1)} %get-tuple-element.8), channel_id=1, source_target_pairs={{128,0},{136,8},{144,16},{152,24},{160,32},{168,40},{176,48},{184,... | collective-permute-start | bytes 393224 | tf_op jit(solution)/shard_map/ppermute | solution.py:12
  429.1 15.0 %collective-permute-start.16 = (f32[64,512]{1,0:T(8,128)S(1)}, f32[64,512]{1,0:T(8,128)S(1)}, u32[]{:S(2)}, u32[]{:S(2)}) collective-permute-start(f32[64,512]{1,0:T(8,128)S(1)} %get-tuple-element.5), channel_id=1, source_target_pairs={{0,256},{8,264},{16,272},{24,280},{32,288},{40,296},{48,304},{56,3... | collective-permute-start | bytes 393224 | tf_op jit(solution)/shard_map/ppermute | solution.py:12
  441.5 17.4 %collective-permute-start.17 = (f32[64,512]{1,0:T(8,128)S(1)}, f32[64,512]{1,0:T(8,128)S(1)}, u32[]{:S(2)}, u32[]{:S(2)}) collective-permute-start(f32[64,512]{1,0:T(8,128)S(1)} %get-tuple-element.6), channel_id=1, source_target_pairs={{256,0},{264,8},{272,16},{280,24},{288,32},{296,40},{304,48},{312,... | collective-permute-start | bytes 393224 | tf_op jit(solution)/shard_map/ppermute | solution.py:12
Sparse Core Ops, SparseCore 0:
  9.5 36.8 all-gather.9
  57.1 34.6 all-gather.11
  102.3 34.6 all-gather.13
  147.9 34.6 all-gather.15
  194.9 34.2 all-gather.17
  244.6 32.4 all-gather.19
  289.5 32.4 all-gather.21
  340.1 30.4 all-gather.23
  399.7 27.2 all-gather.25
where the time goes:
time: 470 us; the launch traced here: 466 us
  waiting for transfers between devices  370 us (79%)
  starting transfers between devices  54.8 us (12%)
  matrix products  18.8 us (4%)
  between operations  13.6 us (3%)
  other arithmetic  6.27 us (1%)
    all_gather x9, waiting for transfers between devices, level_products(): lax.all_gather(current, 'rows', axis=0, tiled=True)  298 us
    ppermute x18, waiting for transfers between devices, from_behind(): lax.ppermute(value, axis, [(source, source + steps) for source in range(f...  70.8 us
    ppermute x18, starting transfers between devices, from_behind(): lax.ppermute(value, axis, [(source, source + steps) for source in range(f...  54.5 us
    dot_general x9, matrix products, level_products(): jnp.dot(window, lax.all_gather(current, 'rows', axis=0, tiled=True), prec...  18.8 us
  transfers between devices with their start and end apart: 27, of which 24 were waited for; matrix products, arithmetic and copies ran while one was open for 1% of the time, Pallas kernels for 0%

commit v1 on v0

v1 whole, which is shorter than its diff:
```python
import functools

import jax
import jax.numpy as jnp
from jax import lax
from jax.experimental import pallas as pl
from jax.experimental.pallas import tpu as pltpu
from jax.sharding import PartitionSpec as P

MESH = pl.DeviceIdType.MESH
F32 = jnp.float32
BF16 = jnp.bfloat16
NX = 4


def shift_down(v, by):
    n, w = v.shape
    if by % 8 == 0:
        return jnp.concatenate((jnp.zeros((by, w), v.dtype), v[: n - by]), axis=0)
    rows = lax.broadcasted_iota(jnp.int32, v.shape, 0)
    return jnp.where(rows < by, 0.0, pltpu.roll(v, by, 0))


def shift_up(v, by):
    n, w = v.shape
    if by % 8 == 0:
        return jnp.concatenate((v[by:], jnp.zeros((by, w), v.dtype)), axis=0)
    rows = lax.broadcasted_iota(jnp.int32, v.shape, 0)
    return jnp.where(rows >= n - by, 0.0, pltpu.roll(v, n - by, 0))


def dot_t(a, b):
    return lax.dot_general(a, b, (((1,), (1,)), ((), ())), preferred_element_type=F32)


def kernel(
    n_chain, levels, groups,
    rhs, diag, left_f, right_f, out,
    x2, src, g0, G, fraw, fhi, flo, ghi, glo, prod, hs, hx, obuf, back, bdst, tb, zb,
    loc_sem, fsend_sem, frecv_sem, pair_send, pair_recv, a2a_send, a2a_recv, ag_send, ag_recv,
):
    C = n_chain
    dev_rows = rhs.shape[0]
    R = 2 * dev_rows
    n_half = src.shape[1]
    Q = C * n_half
    Qs = Q // 2
    hq = Qs // 2
    chain = lax.axis_index("chain")
    rows = lax.axis_index("rows")
    core = lax.rem(rows, 2)
    x = rows // 2
    partner = (chain, x * 2 + (1 - core))
    right = (chain, lax.rem(x + 1, NX) * 2 + core)
    left = (chain, lax.rem(x + NX - 1, NX) * 2 + core)
    facs = (diag, left_f, right_f)

    def local_factor(g, f):
        lo, hi = groups[g]
        return pltpu.make_async_copy(
            facs[f].at[lo:hi], fraw.at[f, lo:hi, core], loc_sem.at[g, f]
        )

    for g in range(len(groups)):
        for f in range(3):
            local_factor(g, f).start()

    barrier = pltpu.get_barrier_semaphore()
    for dev in (partner, right, left):
        pl.semaphore_signal(barrier, inc=1, device_id=dev, device_id_type=MESH)

    def greet(step, carry):
        peer = lax.rem(chain + step, C)
        pl.semaphore_signal(barrier, inc=1, device_id=(peer, rows), device_id_type=MESH)
        return carry

    lax.fori_loop(1, C, greet, 0)
    pl.semaphore_wait(barrier, C - 1 + 3)

    def pair_copy(k, source, target):
        return pltpu.make_async_remote_copy(
            src_ref=source, dst_ref=target, send_sem=pair_send.at[k], recv_sem=pair_recv.at[k],
            device_id=partner, device_id_type=MESH,
        )

    swap = pair_copy(0, rhs, x2.at[core])
    swap.start()

    def remote_factor(g, f):
        lo, hi = groups[g]
        return pltpu.make_async_remote_copy(
            src_ref=facs[f].at[lo:hi], dst_ref=fraw.at[f, lo:hi, core],
            send_sem=fsend_sem.at[g, f], recv_sem=frecv_sem.at[g, f],
            device_id=partner, device_id_type=MESH,
        )

    for g in range(len(groups)):
        for f in range(3):
            remote_factor(g, f).start()

    x2[core] = rhs[...]
    swap.wait()

    for m in range(n_half):
        piece = x2[:, :, m * 2 * C : (m + 1) * 2 * C].reshape(R, 2 * C)
        turned = jnp.transpose(piece)
        src[:, m, :] = jnp.where(core == 0, turned[:C], turned[C:])

    def exchange(k, source, target):
        mine = pltpu.make_async_copy(source.at[chain], target.at[chain], a2a_recv.at[k])
        mine.start()

        def go(step, carry):
            peer = lax.rem(chain + step, C)
            pltpu.make_async_remote_copy(
                src_ref=source.at[peer], dst_ref=target.at[chain],
                send_sem=a2a_send.at[k], recv_sem=a2a_recv.at[k],
                device_id=(peer, rows), device_id_type=MESH,
            ).start()
            return carry

        lax.fori_loop(1, C, go, 0)

    def exchange_wait(k, target):
        pltpu.make_async_copy(target, target, a2a_recv.at[k]).wait()

    def exchange_sent(k, source):
        part = source.at[pl.ds(0, C - 1)]
        pltpu.make_async_copy(part, part, a2a_send.at[k]).wait()

    exchange(0, src, g0)

    def factors_here(g):
        for f in range(3):
            local_factor(g, f).wait()
            remote_factor(g, f).wait_recv()

    def prepare(level):
        for g, (lo, _) in enumerate(groups):
            if lo == level:
                factors_here(g)
        for f in range(3):
            for rel in range(NX):
                at = pl.multiple_of(lax.rem(x + NX - (0, 1, 2, 3)[rel], NX) * R, R)
                v = fraw[f, level, :, :, pl.ds(at, R)].reshape(R, R)
                hi = v.astype(BF16)
                fhi[level, f * R : (f + 1) * R, rel * R : (rel + 1) * R] = hi
                flo[level, f * R : (f + 1) * R, rel * R : (rel + 1) * R] = (v - hi.astype(F32)).astype(BF16)

    halves = (pl.ds(0, hq), pl.ds(hq, hq))

    route = (
        (0, 1, 0, right),
        (0, 3, 1, left),
        (0, 1, 1, right),
        (0, 3, 0, left),
        (1, 2, 0, right),
        (3, 2, 1, left),
    )

    def hop(level, t, k):
        from_slot, to_slot, half, dev = route[k]
        return pltpu.make_async_remote_copy(
            src_ref=G.at[level, t, from_slot, halves[half]],
            dst_ref=G.at[level, t, to_slot, halves[half]],
            send_sem=ag_send.at[level, t], recv_sem=ag_recv.at[level, t, k],
            device_id=dev, device_id_type=MESH,
        )

    def send(level, t):
        for k in range(4):
            hop(level, t, k).start()

    def forward(level, t):
        for k in range(2):
            hop(level, t, k).wait_recv()
            hop(level, t, k + 4).start()

    def sent(level, t):
        part = G.at[level, t, pl.ds(0, 3)]
        pltpu.make_async_copy(part, part, ag_send.at[level, t]).wait()

    def products(level, t):
        for k in (2, 3, 4, 5):
            hop(level, t, k).wait_recv()
        for rel in range(NX):
            v = G[level, t, rel]
            hi = v.astype(BF16)
            ghi[t, :, rel * R : (rel + 1) * R] = hi
            glo[t, :, rel * R : (rel + 1) * R] = (v - hi.astype(F32)).astype(BF16)
        a, b = ghi[t], fhi[level]
        return dot_t(a, b) + dot_t(glo[t], b) + dot_t(a, flo[level])

    prepare(0)
    prepare(1)
    exchange_wait(0, g0)
    for t in range(2):
        for m in range(n_half):
            G[0, t, 0, pl.ds(m, C // 2, stride=n_half), :] = g0[t * (C // 2) : (t + 1) * (C // 2), m, :]
        send(0, t)
    forward(0, 0)
    forward(0, 1)
    for t in range(2):
        prod[t * Qs : (t + 1) * Qs, :] = products(0, t)
    lp = prod[:, R : 2 * R]
    rp = prod[:, 2 * R :]
    hs[...] = jnp.where(core == 0, lp + shift_up(rp, 1), shift_down(lp, 1) + rp)
    other = pair_copy(1, hs, hx)
    other.start()
    prepare(2)
    other.wait()
    new = prod[:, :R] - hx[...]
    for t in range(2):
        G[1, t, 0] = new[t * Qs : (t + 1) * Qs]
        send(1, t)

    prepare(3)
    forward(1, 0)
    forward(1, 1)
    for t in range(2):
        prod[t * Qs : (t + 1) * Qs, :] = products(1, t)
    obuf[...] = prod[:, :R] - shift_down(prod[:, R : 2 * R], 1) - shift_up(prod[:, 2 * R :], 1)
    for t in range(2):
        G[2, t, 0] = obuf[pl.ds(t, Qs, stride=2), :]
        send(2, t)

    def finish(level, t):
        p = products(level, t)
        by = 2 ** (level - 2)
        new = p[:, :R] - shift_down(p[:, R : 2 * R], by) - shift_up(p[:, 2 * R :], by)
        if level + 1 < levels:
            G[level + 1, t, 0] = new
            send(level + 1, t)
        else:
            obuf[t * Qs : (t + 1) * Qs, :] = new
            back[:, t, :] = obuf[pl.ds(t * Qs, C, stride=2), :]
            back[:, 2 + t, :] = obuf[pl.ds(t * Qs + 1, C, stride=2), :]

    forward(2, 0)
    forward(2, 1)
    for level in range(2, levels):
        if level + 2 < levels:
            prepare(level + 2)
        finish(level, 0)
        if level + 1 < levels:
            forward(level + 1, 0)
        finish(level, 1)
        if level + 1 < levels:
            forward(level + 1, 1)

    exchange(1, back, bdst)
    for level in range(levels):
        for t in range(2):
            sent(level, t)
    for g in range(len(groups)):
        for f in range(3):
            remote_factor(g, f).wait_send()
    exchange_sent(0, src)
    exchange_wait(1, bdst)
    for m in range(n_half):
        tb[m] = jnp.transpose(bdst[:, m, :])
    away = pl.ds(pl.multiple_of((1 - core) * dev_rows, dev_rows), dev_rows)
    home = pl.ds(pl.multiple_of(core * dev_rows, dev_rows), dev_rows)
    last = pair_copy(2, tb.at[:, away], zb)
    last.start()
    exchange_sent(1, back)
    last.wait()
    for m in range(n_half):
        own = tb[m, home]
        got = zb[m]
        out[:, m * 2 * C : m * 2 * C + C] = jnp.where(core == 0, own, got)
        out[:, m * 2 * C + C : (m + 1) * 2 * C] = jnp.where(core == 0, got, own)


def solution(mesh):
    n_chain, n_rows = mesh.shape["chain"], mesh.shape["rows"]
    assert n_rows == 2 * NX

    def on_device(rhs, diag, left_f, right_f):
        levels, dev_rows, M = diag.shape
        n_half = rhs.shape[1] // n_chain // 2
        C, R = n_chain, 2 * dev_rows
        Q = C * n_half
        Qs = Q // 2
        groups = ((0, 1), (1, 3), (3, levels))
        scratch = [
            pltpu.VMEM((2,) + rhs.shape, F32),
            pltpu.VMEM((C, n_half, R), F32),
            pltpu.VMEM((C, n_half, R), F32),
            pltpu.VMEM((levels, 2, NX, Qs, R), F32),
            pltpu.VMEM((3, levels, 2, dev_rows, M), F32),
            pltpu.VMEM((levels, 3 * R, M), BF16),
            pltpu.VMEM((levels, 3 * R, M), BF16),
            pltpu.VMEM((2, Qs, M), BF16),
            pltpu.VMEM((2, Qs, M), BF16),
            pltpu.VMEM((Q, 3 * R), F32),
            pltpu.VMEM((Q, R), F32),
            pltpu.VMEM((Q, R), F32),
            pltpu.VMEM((Q, R), F32),
            pltpu.VMEM((C, n_half, R), F32),
            pltpu.VMEM((C, n_half, R), F32),
            pltpu.VMEM((n_half, R, C), F32),
            pltpu.VMEM((n_half, dev_rows, C), F32),
            pltpu.SemaphoreType.DMA((len(groups), 3)),
            pltpu.SemaphoreType.DMA((len(groups), 3)),
            pltpu.SemaphoreType.DMA((len(groups), 3)),
            pltpu.SemaphoreType.DMA((3,)),
            pltpu.SemaphoreType.DMA((3,)),
            pltpu.SemaphoreType.DMA((2,)),
            pltpu.SemaphoreType.DMA((2,)),
            pltpu.SemaphoreType.DMA((levels, 2)),
            pltpu.SemaphoreType.DMA((levels, 2, 6)),
        ]
        vm = pl.BlockSpec(memory_space=pltpu.VMEM)
        hbm = pl.BlockSpec(memory_space=pl.ANY)
        return pl.pallas_call(
            functools.partial(kernel, n_chain, levels, groups),
            out_shape=jax.ShapeDtypeStruct(rhs.shape, F32),
            in_specs=[vm, hbm, hbm, hbm],
            out_specs=vm,
            scratch_shapes=scratch,
            compiler_params=pltpu.CompilerParams(
                collective_id=0, has_side_effects=True, vmem_limit_bytes=48 * 2**20
            ),
        )(rhs, diag, left_f, right_f)

    placed = (
        P("rows", "chain"),
        P(None, "rows", None),
        P(None, "rows", None),
        P(None, "rows", None),
    )
    return jax.shard_map(
        on_device, mesh=mesh, in_specs=placed, out_specs=P("rows", "chain"), check_vma=False
    )
```

time: 470 us -> 137 us (0.29)
  waiting for transfers between devices: 370 us -> 0 us
  Pallas kernels: 0 us -> 131 us
  starting transfers between devices: 54.8 us -> 0 us
  matrix products: 18.8 us -> 0 us
  between operations: 13.6 us -> 0.01 us
  other arithmetic: 6.27 us -> 0 us
    all_gather x9 -> x0, waiting for transfers between devices: 298 us -> none  [level_products(): lax.all_gather(current, 'rows', axis=0, tiled=True)]
    pallas_call x0 -> x1, Pallas kernels: none -> 131 us  [on_device(): pl.pallas_call(functools.partial(kernel, n_chain, levels, groups), out_sh...]
    ppermute x18 -> x0, waiting for transfers between devices: 70.8 us -> none  [from_behind(): lax.ppermute(value, axis, [(source, source + steps) for source in range(f...]
    ppermute x18 -> x0, starting transfers between devices: 54.5 us -> none  [from_behind(): lax.ppermute(value, axis, [(source, source + steps) for source in range(f...]
    dot_general x9 -> x0, matrix products: 18.8 us -> none  [level_products(): jnp.dot(window, lax.all_gather(current, 'rows', axis=0, tiled=True), prec...]
    sub x9 -> x0, other arithmetic: 6.27 us -> none  [on_device(): current = own_term - left_in - right_in]
  transfers between devices with their start and end apart: 27 -> 0, of which waited for: 24 -> 0; matrix products, arithmetic and copies ran while one was open for 1% -> 0% of each run, Pallas kernels for 0% -> 0%
where the time goes in v1:
time: 137 us
  Pallas kernels  131 us (96%)
  local copies, waits for them, and re-layouts  5.37 us (4%)
    pallas_call x1, Pallas kernels, on_device(): pl.pallas_call(functools.partial(kernel, n_chain, levels, groups), out_sh...  131 us
    unnamed x9, local copies, waits for them, and re-layouts  5.37 us

profile of v1, /device:TPU:1, one launch (start us, length us, event | category | flops | bytes accessed | tf_op | source)
XLA Modules:
  0.0 136.7 jit_solution(10041715311963423925)
XLA Ops:
  0.0 0.0 copy-start
  0.0 1.3 copy-done
  1.3 0.0 copy-start.1
  1.3 1.3 copy-done.1
  2.5 0.0 copy-start.2
  2.5 1.3 copy-done.2
  3.8 0.0 copy-start.3
  3.8 0.9 copy-done.3
  4.7 131.3 %shard_map.46 = f32[64,512]{1,0:T(8,128)S(1)} custom-call(f32[64,512]{1,0:T(8,128)S(1)} %copy-done.3, f32[9,64,512]{2,1,0:T(8,128)S(1)} %copy-done, f32[9,64,512]{2,1,0:T(8,128)S(1)} %copy-done.1, f32[9,64,512]{2,1,0:T(8,128)S(1)} %copy-done.2), custom_call_target="tpu_custom_call" | custom-call | tf_op jit(solution)/shard_map/pallas_call | solution.py:316
  136.1 0.7 copy.6
Async XLA Ops:
  0.0 1.3 copy-start
  1.3 1.3 copy-start.1
  2.5 1.3 copy-start.2
  3.8 0.9 copy-start.3

commit v2 on v1

v2 whole, which is shorter than its diff:
```python
import functools

import jax
import jax.numpy as jnp
from jax import lax
from jax.experimental import pallas as pl
from jax.experimental.pallas import tpu as pltpu
from jax.sharding import PartitionSpec as P

MESH = pl.DeviceIdType.MESH
F32 = jnp.float32
BF16 = jnp.bfloat16
NX = 4
NY = 4


def shift_down(v, by):
    n, w = v.shape
    if by % 8 == 0:
        return jnp.concatenate((jnp.zeros((by, w), v.dtype), v[: n - by]), axis=0)
    rows = lax.broadcasted_iota(jnp.int32, v.shape, 0)
    return jnp.where(rows < by, 0.0, pltpu.roll(v, by, 0))


def shift_up(v, by):
    n, w = v.shape
    if by % 8 == 0:
        return jnp.concatenate((v[by:], jnp.zeros((by, w), v.dtype)), axis=0)
    rows = lax.broadcasted_iota(jnp.int32, v.shape, 0)
    return jnp.where(rows >= n - by, 0.0, pltpu.roll(v, n - by, 0))


def dot_t(a, b):
    return lax.dot_general(a, b, (((1,), (1,)), ((), ())), preferred_element_type=F32)


def kernel(
    n_chain, levels, groups,
    rhs, diag, left_f, right_f, out,
    x2, src, ybuf, g0, G, fraw, fhi, flo, ghi, glo, prod, hs, hx, obuf, back, zbuf, bdst, turn, tb, zb,
    loc_sem, fsend_sem, frecv_sem, pair_send, pair_recv, a2a_send, a2a_recv, ag_send, ag_recv, own_sem, known,
):
    C = n_chain
    nz = C // NY
    dev_rows = rhs.shape[0]
    R = 2 * dev_rows
    n_half = src.shape[2]
    Q = C * n_half
    Qs = Q // 2
    chain = lax.axis_index("chain")
    rows = lax.axis_index("rows")
    core = lax.rem(rows, 2)
    x = rows // 2
    y = lax.rem(chain, NY)
    z = chain // NY
    partner = (chain, x * 2 + (1 - core))
    right = (chain, lax.rem(x + 1, NX) * 2 + core)
    left = (chain, lax.rem(x + NX - 1, NX) * 2 + core)
    across = (chain, lax.rem(x + 2, NX) * 2 + core)
    facs = (diag, left_f, right_f)

    def z_of(by):
        return lax.rem(z + by + nz, nz)

    def y_of(by):
        return lax.rem(y + by, NY)

    def z_dev(by):
        return (z_of(by) * NY + y, rows)

    def y_dev(by):
        return (z * NY + y_of(by), rows)

    def both_ways(by):
        return (by,) if 2 * by == nz else (by, -by)

    def signal(sem, dev):
        pl.semaphore_signal(sem, inc=1, device_id=dev, device_id_type=MESH)

    barrier = pltpu.get_barrier_semaphore()
    near = [partner, right, left, across] + [z_dev(b) for b in both_ways(1)] + [y_dev(b) for b in range(1, NY)]
    for dev in near:
        signal(barrier, dev)

    def local_factor(g, f):
        lo, hi = groups[g]
        return pltpu.make_async_copy(
            facs[f].at[lo:hi], fraw.at[f, lo:hi, core], loc_sem.at[g, f]
        )

    own_rhs = pltpu.make_async_copy(rhs, x2.at[core], own_sem)
    own_rhs.start()
    for g in range(len(groups)):
        for f in range(3):
            local_factor(g, f).start()

    pl.semaphore_wait(barrier, len(near))

    def pair_copy(k, source, target):
        return pltpu.make_async_remote_copy(
            src_ref=source, dst_ref=target, send_sem=pair_send.at[k], recv_sem=pair_recv.at[k],
            device_id=partner, device_id_type=MESH,
        )

    swap = pair_copy(0, rhs, x2.at[core])
    swap.start()

    rounds = max(0, nz.bit_length() - 2)

    def tell(k):
        if k < rounds:
            for b in both_ways(2**k):
                signal(known.at[k], z_dev(b))

    def told(k):
        if k < rounds:
            pl.semaphore_wait(known.at[k], len(both_ways(2**k)))

    tell(0)

    def remote_factor(g, f):
        lo, hi = groups[g]
        return pltpu.make_async_remote_copy(
            src_ref=facs[f].at[lo:hi], dst_ref=fraw.at[f, lo:hi, core],
            send_sem=fsend_sem.at[g, f], recv_sem=frecv_sem.at[g, f],
            device_id=partner, device_id_type=MESH,
        )

    for f in range(3):
        remote_factor(0, f).start()

    told(0)
    tell(1)
    own_rhs.wait()
    swap.wait()

    for m in range(n_half):
        piece = x2[:, :, m * 2 * C : (m + 1) * 2 * C].reshape(R, 2 * C)
        turned = jnp.transpose(piece)
        mine = jnp.where(core == 0, turned[:C], turned[C:])
        for cz in range(nz):
            src[cz, :, m, :] = mine[cz * NY : (cz + 1) * NY]

    def phase(k, source, target, mine, others):
        own = pltpu.make_async_copy(source(mine), target.at[mine], a2a_recv.at[k])
        for place, dev in others:
            pltpu.make_async_remote_copy(
                src_ref=source(place), dst_ref=target.at[mine],
                send_sem=a2a_send.at[k], recv_sem=a2a_recv.at[k],
                device_id=dev, device_id_type=MESH,
            ).start()
        own.start()

    def landed(k, target):
        pltpu.make_async_copy(target, target, a2a_recv.at[k]).wait()

    def gone(k, part):
        pltpu.make_async_copy(part, part, a2a_send.at[k]).wait()

    y_others = [(y_of(b), y_dev(b)) for b in range(1, NY)]
    z_others = []
    for b in range(nz // 2, 0, -1):
        for by in both_ways(b):
            z_others.append((z_of(by), z_dev(by)))

    phase(0, lambda p: src.at[:, p], ybuf, y, y_others)
    told(1)
    tell(2)
    for g in range(1, len(groups)):
        for f in range(3):
            remote_factor(g, f).start()
    landed(0, ybuf)
    for k in range(2, rounds):
        told(k)
        tell(k + 1)
    phase(1, lambda p: ybuf.at[:, p], g0, z, z_others)

    def factors_here(g):
        for f in range(3):
            local_factor(g, f).wait()
            remote_factor(g, f).wait_recv()

    def prepare(level):
        for g, (lo, _) in enumerate(groups):
            if lo == level:
                factors_here(g)
        for f in range(3):
            for rel in range(NX):
                at = pl.multiple_of(lax.rem(x + NX - rel, NX) * R, R)
                v = fraw[f, level, :, :, pl.ds(at, R)].reshape(R, R)
                hi = v.astype(BF16)
                fhi[level, f * R : (f + 1) * R, rel * R : (rel + 1) * R] = hi
                flo[level, f * R : (f + 1) * R, rel * R : (rel + 1) * R] = (v - hi.astype(F32)).astype(BF16)

    route = ((2, across), (1, right), (3, left))

    def hop(level, t, k):
        slot, dev = route[k]
        return pltpu.make_async_remote_copy(
            src_ref=G.at[level, t, 0], dst_ref=G.at[level, t, slot],
            send_sem=ag_send.at[level, t], recv_sem=ag_recv.at[level, t, k],
            device_id=dev, device_id_type=MESH,
        )

    def send(level, t):
        for k in range(3):
            hop(level, t, k).start()

    def sent(level, t):
        part = G.at[level, t, pl.ds(0, 3)]
        pltpu.make_async_copy(part, part, ag_send.at[level, t]).wait()

    def part(level, t, first):
        for rel in (first, first + 1):
            v = G[level, t, rel]
            hi = v.astype(BF16)
            ghi[t, :, rel * R : (rel + 1) * R] = hi
            glo[t, :, rel * R : (rel + 1) * R] = (v - hi.astype(F32)).astype(BF16)
        ks = slice(first * R, (first + 2) * R)
        a, b = ghi[t, :, ks], fhi[level, :, ks]
        return dot_t(a, b) + dot_t(glo[t, :, ks], b) + dot_t(a, flo[level, :, ks])

    def early(level, t):
        hop(level, t, 1).wait_recv()
        prod[t * Qs : (t + 1) * Qs, :] = part(level, t, 0)

    def late(level, t):
        for k in (2, 0):
            hop(level, t, k).wait_recv()
        return prod[t * Qs : (t + 1) * Qs, :] + part(level, t, 2)

    def both(level):
        for t in range(2):
            early(level, t)
        for t in range(2):
            prod[t * Qs : (t + 1) * Qs, :] = late(level, t)

    prepare(0)
    landed(1, g0)
    for t in range(2):
        for c in range(C // 2):
            G[0, t, 0, c * n_half : (c + 1) * n_half, :] = g0[(t * (C // 2) + c) // NY, c % NY]
        send(0, t)
    prepare(1)
    both(0)
    lp = prod[:, R : 2 * R]
    rp = prod[:, 2 * R :]
    hs[...] = jnp.where(core == 0, lp + shift_up(rp, 1), shift_down(lp, 1) + rp)
    other = pair_copy(1, hs, hx)
    other.start()
    prepare(2)
    other.wait()
    new = prod[:, :R] - hx[...]
    for t in range(2):
        G[1, t, 0] = new[t * Qs : (t + 1) * Qs]
        send(1, t)

    prepare(3)
    both(1)
    obuf[...] = prod[:, :R] - shift_down(prod[:, R : 2 * R], 1) - shift_up(prod[:, 2 * R :], 1)
    for t in range(2):
        G[2, t, 0] = obuf[pl.ds(t, Qs, stride=2), :]
        send(2, t)

    def finish(level, t):
        early(level, t)
        p = late(level, t)
        by = 2 ** (level - 2)
        new = p[:, :R] - shift_down(p[:, R : 2 * R], by) - shift_up(p[:, 2 * R :], by)
        if level + 1 < levels:
            G[level + 1, t, 0] = new
            send(level + 1, t)
        else:
            obuf[pl.ds(t, Qs, stride=2), :] = new

    for level in range(2, levels):
        if level + 2 < levels:
            prepare(level + 2)
        finish(level, 0)
        finish(level, 1)

    for c in range(C):
        back[c // NY, c % NY] = obuf[c * n_half : (c + 1) * n_half, :]
    phase(2, lambda p: back.at[p], zbuf, z, z_others)
    for level in range(levels):
        for t in range(2):
            sent(level, t)
    for g in range(len(groups)):
        for f in range(3):
            remote_factor(g, f).wait_send()
    gone(0, src.at[:, pl.ds(0, NY - 1)])
    gone(1, ybuf.at[:, pl.ds(0, nz - 1)])
    landed(2, zbuf)
    phase(3, lambda p: zbuf.at[:, p], bdst, y, y_others)
    gone(2, back.at[pl.ds(0, nz - 1)])
    landed(3, bdst)
    for m in range(n_half):
        for cy in range(NY):
            turn[m, pl.ds(cy, nz, stride=NY), :] = bdst[cy, :, m, :]
        tb[m] = jnp.transpose(turn[m])
    away = pl.ds(pl.multiple_of((1 - core) * dev_rows, dev_rows), dev_rows)
    home = pl.ds(pl.multiple_of(core * dev_rows, dev_rows), dev_rows)
    last = pair_copy(2, tb.at[:, away], zb)
    last.start()
    gone(3, zbuf.at[:, pl.ds(0, NY - 1)])
    last.wait()
    for m in range(n_half):
        own = tb[m, home]
        got = zb[m]
        out[:, m * 2 * C : m * 2 * C + C] = jnp.where(core == 0, own, got)
        out[:, m * 2 * C + C : (m + 1) * 2 * C] = jnp.where(core == 0, got, own)


def solution(mesh):
    n_chain, n_rows = mesh.shape["chain"], mesh.shape["rows"]
    assert n_rows == 2 * NX and n_chain % NY == 0

    def on_device(rhs, diag, left_f, right_f):
        levels, dev_rows, M = diag.shape
        n_half = rhs.shape[1] // n_chain // 2
        C, R = n_chain, 2 * dev_rows
        nz = C // NY
        Q = C * n_half
        Qs = Q // 2
        groups = ((0, 1), (1, 3), (3, levels))
        scratch = [
            pltpu.VMEM((2,) + rhs.shape, F32),
            pltpu.VMEM((nz, NY, n_half, R), F32),
            pltpu.VMEM((NY, nz, n_half, R), F32),
            pltpu.VMEM((nz, NY, n_half, R), F32),
            pltpu.VMEM((levels, 2, NX, Qs, R), F32),
            pltpu.VMEM((3, levels, 2, dev_rows, M), F32),
            pltpu.VMEM((levels, 3 * R, M), BF16),
            pltpu.VMEM((levels, 3 * R, M), BF16),
            pltpu.VMEM((2, Qs, M), BF16),
            pltpu.VMEM((2, Qs, M), BF16),
            pltpu.VMEM((Q, 3 * R), F32),
            pltpu.VMEM((Q, R), F32),
            pltpu.VMEM((Q, R), F32),
            pltpu.VMEM((Q, R), F32),
            pltpu.VMEM((nz, NY, n_half, R), F32),
            pltpu.VMEM((nz, NY, n_half, R), F32),
            pltpu.VMEM((NY, nz, n_half, R), F32),
            pltpu.VMEM((n_half, C, R), F32),
            pltpu.VMEM((n_half, R, C), F32),
            pltpu.VMEM((n_half, dev_rows, C), F32),
            pltpu.SemaphoreType.DMA((len(groups), 3)),
            pltpu.SemaphoreType.DMA((len(groups), 3)),
            pltpu.SemaphoreType.DMA((len(groups), 3)),
            pltpu.SemaphoreType.DMA((3,)),
            pltpu.SemaphoreType.DMA((3,)),
            pltpu.SemaphoreType.DMA((4,)),
            pltpu.SemaphoreType.DMA((4,)),
            pltpu.SemaphoreType.DMA((levels, 2)),
            pltpu.SemaphoreType.DMA((levels, 2, 3)),
            pltpu.SemaphoreType.DMA,
            pltpu.SemaphoreType.REGULAR((3,)),
        ]
        vm = pl.BlockSpec(memory_space=pltpu.VMEM)
        hbm = pl.BlockSpec(memory_space=pl.ANY)
        return pl.pallas_call(
            functools.partial(kernel, n_chain, levels, groups),
            out_shape=jax.ShapeDtypeStruct(rhs.shape, F32),
            in_specs=[hbm, hbm, hbm, hbm],
            out_specs=vm,
            scratch_shapes=scratch,
            compiler_params=pltpu.CompilerParams(
                collective_id=0, has_side_effects=True, vmem_limit_bytes=63 * 2**20
            ),
        )(rhs, diag, left_f, right_f)

    placed = (
        P("rows", "chain"),
        P(None, "rows", None),
        P(None, "rows", None),
        P(None, "rows", None),
    )
    return jax.shard_map(
        on_device, mesh=mesh, in_specs=placed, out_specs=P("rows", "chain"), check_vma=False
    )
```

time: 137 us -> 108 us (0.79)
  Pallas kernels: 131 us -> 107 us
  local copies, waits for them, and re-layouts: 5.37 us -> 1.57 us
    pallas_call x1, Pallas kernels: 131 us -> 107 us  [on_device(): pl.pallas_call(functools.partial(kernel, n_chain, levels, groups), out_sh...]
    unnamed x9 -> x1, local copies, waits for them, and re-layouts: 5.37 us -> 1.57 us
where the time goes in v2:
time: 108 us
  Pallas kernels  107 us (99%)
  local copies, waits for them, and re-layouts  1.57 us (1%)
    pallas_call x1, Pallas kernels, on_device(): pl.pallas_call(functools.partial(kernel, n_chain, levels, groups), out_sh...  107 us

profile of v2, /device:TPU:1, one launch (start us, length us, event | category | flops | bytes accessed | tf_op | source)
XLA Modules:
  0.0 108.2 jit_solution(18055701986205181536)
XLA Ops:
  0.0 106.6 %shard_map.46 = f32[64,512]{1,0:T(8,128)} custom-call(f32[64,512]{1,0:T(8,128)} %rhs.1, f32[9,64,512]{2,1,0:T(8,128)} %diag.1, f32[9,64,512]{2,1,0:T(8,128)} %left_f.1, f32[9,64,512]{2,1,0:T(8,128)} %right_f.1), custom_call_target="tpu_custom_call" | custom-call | tf_op jit(solution)/shard_map/pallas_call | solution.py:361
  106.6 1.6 %copy.6 = f32[64,512]{1,0:T(8,128)} copy(f32[64,512]{1,0:T(8,128)} %shard_map.46) | data formatting | bytes 262144

commit v3 on v2

v3 whole, which is shorter than its diff:
```python
import functools

import jax
import jax.numpy as jnp
from jax import lax
from jax.experimental import pallas as pl
from jax.experimental.pallas import tpu as pltpu
from jax.sharding import PartitionSpec as P

MESH = pl.DeviceIdType.MESH
F32 = jnp.float32
BF16 = jnp.bfloat16
NX = 4
NY = 4
HALO = 8


def shift_down(v, by):
    n, w = v.shape
    if by % 8 == 0:
        return jnp.concatenate((jnp.zeros((by, w), v.dtype), v[: n - by]), axis=0)
    rows = lax.broadcasted_iota(jnp.int32, v.shape, 0)
    return jnp.where(rows < by, 0.0, pltpu.roll(v, by, 0))


def shift_up(v, by):
    n, w = v.shape
    if by % 8 == 0:
        return jnp.concatenate((v[by:], jnp.zeros((by, w), v.dtype)), axis=0)
    rows = lax.broadcasted_iota(jnp.int32, v.shape, 0)
    return jnp.where(rows >= n - by, 0.0, pltpu.roll(v, n - by, 0))


def dot_t(a, b):
    return lax.dot_general(a, b, (((1,), (1,)), ((), ())), preferred_element_type=F32)


def three_pass(v, f_hi, f_lo):
    hi = v.astype(BF16)
    lo = (v - hi.astype(F32)).astype(BF16)
    return dot_t(hi, f_hi) + dot_t(lo, f_hi) + dot_t(hi, f_lo)


def kernel(
    n_chain, levels, groups,
    rhs, diag, left_f, right_f, out,
    x2, src, ybuf, g0, GN, G, fraw, f0hi, f0lo, fhi, flo, ghi, glo, prod, hs, hx, obuf, es, ex, back, zbuf, bdst, turn,
    loc_sem, fsend_sem, frecv_sem, pair_send, pair_recv, a2a_send, a2a_recv, ag_send, ag_recv, l2_recv, own_sem, known,
):
    C = n_chain
    nz = C // NY
    dev_rows = rhs.shape[0]
    R = 2 * dev_rows
    n_half = src.shape[2]
    Q = C * n_half
    Qs = Q // 2
    Qh = Qs + HALO
    chain = lax.axis_index("chain")
    rows = lax.axis_index("rows")
    core = lax.rem(rows, 2)
    x = rows // 2
    y = lax.rem(chain, NY)
    z = chain // NY
    partner = (chain, x * 2 + (1 - core))
    right = (chain, lax.rem(x + 1, NX) * 2 + core)
    left = (chain, lax.rem(x + NX - 1, NX) * 2 + core)
    across = (chain, lax.rem(x + 2, NX) * 2 + core)
    facs = (diag, left_f, right_f)

    def z_of(by):
        return lax.rem(z + by + nz, nz)

    def y_of(by):
        return lax.rem(y + by, NY)

    def z_dev(by):
        return (z_of(by) * NY + y, rows)

    def y_dev(by):
        return (z * NY + y_of(by), rows)

    def both_ways(by):
        return (by,) if 2 * by == nz else (by, -by)

    def signal(sem, dev):
        pl.semaphore_signal(sem, inc=1, device_id=dev, device_id_type=MESH)

    barrier = pltpu.get_barrier_semaphore()
    reach = min(4, nz // 2)
    near = [z_dev(by) for b in range(reach, 0, -1) for by in both_ways(b)]
    near += [y_dev(b) for b in range(1, NY)] + [across, right, left, partner]
    for dev in near:
        signal(barrier, dev)

    def local_factor(g, f):
        lo, hi = groups[g]
        return pltpu.make_async_copy(
            facs[f].at[lo:hi], fraw.at[f, lo:hi, core], loc_sem.at[g, f]
        )

    own_rhs = pltpu.make_async_copy(rhs, x2, own_sem)
    own_rhs.start()
    for g in range(len(groups)):
        for f in range(3):
            local_factor(g, f).start()

    own_rhs.wait()
    for m in range(n_half):
        turned = jnp.transpose(x2[:, m * 2 * C : (m + 1) * 2 * C])
        pairs = jnp.concatenate((turned[:C], turned[C:]), axis=1)
        for cz in range(nz):
            src[cz, :, m, :] = pairs[cz * NY : (cz + 1) * NY]

    pl.semaphore_wait(barrier, len(near))

    far = nz // 2 > reach
    if far:
        for by in both_ways(reach):
            signal(known, z_dev(by))

    def pair_copy(k, source, target):
        return pltpu.make_async_remote_copy(
            src_ref=source, dst_ref=target, send_sem=pair_send.at[k], recv_sem=pair_recv.at[k],
            device_id=partner, device_id_type=MESH,
        )

    def remote_factor(g, f):
        lo, hi = groups[g]
        return pltpu.make_async_remote_copy(
            src_ref=facs[f].at[lo:hi], dst_ref=fraw.at[f, lo:hi, core],
            send_sem=fsend_sem.at[g, f], recv_sem=frecv_sem.at[g, f],
            device_id=partner, device_id_type=MESH,
        )

    def phase(k, source, target, mine, others):
        own = pltpu.make_async_copy(source(mine), target.at[mine], a2a_recv.at[k])
        for place, dev in others:
            pltpu.make_async_remote_copy(
                src_ref=source(place), dst_ref=target.at[mine],
                send_sem=a2a_send.at[k], recv_sem=a2a_recv.at[k],
                device_id=dev, device_id_type=MESH,
            ).start()
        own.start()

    def landed(k, target):
        pltpu.make_async_copy(target, target, a2a_recv.at[k]).wait()

    def gone(k, part):
        pltpu.make_async_copy(part, part, a2a_send.at[k]).wait()

    y_others = [(y_of(b), y_dev(b)) for b in range(1, NY)]
    z_others = []
    for b in range(nz // 2, 0, -1):
        for by in both_ways(b):
            z_others.append((z_of(by), z_dev(by)))

    phase(0, lambda p: src.at[:, p], ybuf, y, y_others)
    for g in range(len(groups)):
        for f in range(3):
            remote_factor(g, f).start()
    landed(0, ybuf)
    if far:
        pl.semaphore_wait(known, 2)
    phase(1, lambda p: ybuf.at[:, p], g0, z, z_others)

    def factors_here(level):
        for g, (lo, _) in enumerate(groups):
            if lo == level:
                for f in range(3):
                    local_factor(g, f).wait()
                    remote_factor(g, f).wait_recv()

    def columns(f, level, rel):
        at = pl.multiple_of(lax.rem(x + NX - rel, NX) * R, R)
        return fraw[f, level, :, :, pl.ds(at, R)].reshape(R, R)

    def prepare(level):
        factors_here(level)
        for f in range(3):
            for rel in range(NX):
                v = columns(f, level, rel)
                hi = v.astype(BF16)
                fhi[level, f * R : (f + 1) * R, rel * R : (rel + 1) * R] = hi
                flo[level, f * R : (f + 1) * R, rel * R : (rel + 1) * R] = (v - hi.astype(F32)).astype(BF16)

    def low(v):
        return lax.broadcasted_iota(jnp.int32, v.shape, 1) < dev_rows

    def turn_lanes(v):
        return pltpu.roll(v, dev_rows, 1)

    def firsts(a, b):
        return jnp.where(low(a), a, turn_lanes(b))

    def seconds(a, b):
        return jnp.where(low(a), turn_lanes(a), b)

    def prepare_first():
        factors_here(0)
        for f in range(3):
            for k in range(NX // 2):
                a, b = columns(f, 0, 2 * k), columns(f, 0, 2 * k + 1)
                v = jnp.where(core == 0, firsts(a, b), seconds(a, b))
                hi = v.astype(BF16)
                f0hi[f * R : (f + 1) * R, k * R : (k + 1) * R] = hi
                f0lo[f * R : (f + 1) * R, k * R : (k + 1) * R] = (v - hi.astype(F32)).astype(BF16)

    route = ((2, across), (1, right), (3, left))

    def chunk(level, t, slot):
        return GN.at[level, t, slot] if level < 2 else G.at[level - 2, t, slot]

    def hop(level, t, k, piece=None):
        slot, dev = route[k]
        source, target, recv = chunk(level, t, 0), chunk(level, t, slot), ag_recv.at[level, t, k]
        if piece is not None:
            some = pl.ds(piece * (Qs // 2), Qs // 2)
            source, target, recv = source.at[some], target.at[some], l2_recv.at[t, piece, k]
        return pltpu.make_async_remote_copy(
            src_ref=source, dst_ref=target, send_sem=ag_send.at[level, t], recv_sem=recv,
            device_id=dev, device_id_type=MESH,
        )

    def send(level, t, piece=None):
        for k in range(3):
            hop(level, t, k, piece).start()

    def arrived(level, t, k):
        if level == 2:
            for piece in range(2):
                hop(level, t, k, piece).wait_recv()
        else:
            hop(level, t, k).wait_recv()

    def sent(level, t):
        part = chunk(level, t, pl.ds(0, 3))
        pltpu.make_async_copy(part, part, ag_send.at[level, t]).wait()

    def padded(v):
        return jnp.concatenate((v, jnp.zeros((HALO, v.shape[1]), F32)), axis=0)

    prepare_first()
    landed(1, g0)
    first = (0, (Qs - HALO) // n_half)
    for t in range(2):
        for i in range(Qh // n_half):
            c = first[t] + i
            GN[0, t, 0, i * n_half : (i + 1) * n_half, :] = g0[c // NY, c % NY]
        send(0, t)
    prepare(1)
    for t in range(2):
        for k in (1, 2, 0):
            arrived(0, t, k)
        a = [GN[0, t, rel] for rel in range(NX)]
        ev = jnp.concatenate((firsts(a[0], a[1]), firsts(a[2], a[3])), axis=1)
        pe = three_pass(padded(ev), f0hi[...], f0lo[...])[:Qh]
        od = jnp.concatenate((seconds(a[0], a[1]), seconds(a[2], a[3])), axis=1)
        po = three_pass(padded(od), f0hi[...], f0lo[...])[:Qh]
        to_even = pe[:, :R] - shift_down(po[:, R : 2 * R], 1) - po[:, 2 * R :]
        to_odd = po[:, :R] - pe[:, R : 2 * R] - shift_up(pe[:, 2 * R :], 1)
        hs[t] = jnp.where(core == 0, to_odd, to_even)
        other = pair_copy(t, hs.at[t], hx.at[t])
        other.start()
        mine = jnp.where(core == 0, to_even, to_odd)
        other.wait_recv()
        GN[1, t, 0] = mine + hx[t]
        send(1, t)

    prepare(2)
    for t in range(2):
        for k in (1, 2, 0):
            arrived(1, t, k)
        v = jnp.concatenate([GN[1, t, rel] for rel in range(NX)], axis=1)
        p = three_pass(padded(v), fhi[1], flo[1])[:Qh]
        new = p[:, :R] - shift_down(p[:, R : 2 * R], 1) - shift_up(p[:, 2 * R :], 1)
        obuf[t] = new[:Qs] if t == 0 else new[HALO:]
        for u in range(2):
            G[0, u, 0, t * (Qs // 2) : (t + 1) * (Qs // 2), :] = obuf[t, pl.ds(u, Qs // 2, stride=2), :]
            send(2, u, t)

    def part(level, t, first):
        for rel in (first, first + 1):
            v = G[level - 2, t, rel]
            hi = v.astype(BF16)
            ghi[t, :, rel * R : (rel + 1) * R] = hi
            glo[t, :, rel * R : (rel + 1) * R] = (v - hi.astype(F32)).astype(BF16)
        ks = slice(first * R, (first + 2) * R)
        a, b = ghi[t, :, ks], fhi[level, :, ks]
        return dot_t(a, b) + dot_t(glo[t, :, ks], b) + dot_t(a, flo[level, :, ks])

    def finish(level, t):
        arrived(level, t, 1)
        prod[t] = part(level, t, 0)
        arrived(level, t, 2)
        arrived(level, t, 0)
        p = prod[t] + part(level, t, 2)
        by = 2 ** (level - 2)
        return p[:, :R] - shift_down(p[:, R : 2 * R], by) - shift_up(p[:, 2 * R :], by)

    for level in range(2, levels - 1):
        prepare(level + 1)
        for t in range(2):
            G[level - 1, t, 0] = finish(level, t)
            send(level + 1, t)

    for t in range(2):
        new = finish(levels - 1, t)
        es[t] = new
        other = pair_copy(2 + t, es.at[t], ex.at[t])
        other.start()
        other.wait_recv()
        got = turn_lanes(ex[t])
        both = jnp.where(low(new) == (core == 0), new, got)
        for c in range(C):
            back[t, c // NY, c % NY] = both[2 * c : 2 * c + 2]
        phase(2 + t, lambda p: back.at[t, p], zbuf.at[t], z, z_others)

    for level in range(levels):
        for t in range(2):
            sent(level, t)
    for g in range(len(groups)):
        for f in range(3):
            remote_factor(g, f).wait_send()
    gone(0, src.at[:, pl.ds(0, NY - 1)])
    gone(1, ybuf.at[:, pl.ds(0, nz - 1)])
    for t in range(2):
        pair_copy(t, hs.at[t], hx.at[t]).wait_send()
        pair_copy(2 + t, es.at[t], ex.at[t]).wait_send()
    for t in range(2):
        landed(2 + t, zbuf.at[t])
        phase(4 + t, lambda p: zbuf.at[t, :, p], bdst.at[t], y, y_others)
    for t in range(2):
        gone(2 + t, back.at[t, pl.ds(0, nz - 1)])
        landed(4 + t, bdst.at[t])
        for j in range(2):
            m = 2 * j + t
            for cy in range(NY):
                turn[m, pl.ds(cy, nz, stride=NY), :] = bdst[t, cy, :, j, :]
            wide = jnp.transpose(turn[m])
            out[:, m * 2 * C : (m + 1) * 2 * C] = jnp.concatenate((wide[:dev_rows], wide[dev_rows:]), axis=1)
    for t in range(2):
        gone(4 + t, zbuf.at[t, :, pl.ds(0, NY - 1)])


def solution(mesh):
    n_chain, n_rows = mesh.shape["chain"], mesh.shape["rows"]
    assert n_rows == 2 * NX and n_chain % NY == 0

    def on_device(rhs, diag, left_f, right_f):
        levels, dev_rows, M = diag.shape
        n_half = rhs.shape[1] // n_chain // 2
        C, R = n_chain, 2 * dev_rows
        nz = C // NY
        Q = C * n_half
        Qs = Q // 2
        Qh = Qs + HALO
        groups = ((0, 1), (1, 3), (3, levels))
        scratch = [
            pltpu.VMEM(rhs.shape, F32),
            pltpu.VMEM((nz, NY, n_half, R), F32),
            pltpu.VMEM((NY, nz, n_half, R), F32),
            pltpu.VMEM((nz, NY, n_half, R), F32),
            pltpu.VMEM((2, 2, NX, Qh, R), F32),
            pltpu.VMEM((levels - 2, 2, NX, Qs, R), F32),
            pltpu.VMEM((3, levels, 2, dev_rows, M), F32),
            pltpu.VMEM((3 * R, M // 2), BF16),
            pltpu.VMEM((3 * R, M // 2), BF16),
            pltpu.VMEM((levels, 3 * R, M), BF16),
            pltpu.VMEM((levels, 3 * R, M), BF16),
            pltpu.VMEM((2, Qs, M), BF16),
            pltpu.VMEM((2, Qs, M), BF16),
            pltpu.VMEM((2, Qs, 3 * R), F32),
            pltpu.VMEM((2, Qh, R), F32),
            pltpu.VMEM((2, Qh, R), F32),
            pltpu.VMEM((2, Qs, R), F32),
            pltpu.VMEM((2, Qs, R), F32),
            pltpu.VMEM((2, Qs, R), F32),
            pltpu.VMEM((2, nz, NY, 2, R), F32),
            pltpu.VMEM((2, nz, NY, 2, R), F32),
            pltpu.VMEM((2, NY, nz, 2, R), F32),
            pltpu.VMEM((n_half, C, R), F32),
            pltpu.SemaphoreType.DMA((len(groups), 3)),
            pltpu.SemaphoreType.DMA((len(groups), 3)),
            pltpu.SemaphoreType.DMA((len(groups), 3)),
            pltpu.SemaphoreType.DMA((4,)),
            pltpu.SemaphoreType.DMA((4,)),
            pltpu.SemaphoreType.DMA((6,)),
            pltpu.SemaphoreType.DMA((6,)),
            pltpu.SemaphoreType.DMA((levels, 2)),
            pltpu.SemaphoreType.DMA((levels, 2, 3)),
            pltpu.SemaphoreType.DMA((2, 2, 3)),
            pltpu.SemaphoreType.DMA,
            pltpu.SemaphoreType.REGULAR,
        ]
        vm = pl.BlockSpec(memory_space=pltpu.VMEM)
        hbm = pl.BlockSpec(memory_space=pl.ANY)
        return pl.pallas_call(
            functools.partial(kernel, n_chain, levels, groups),
            out_shape=jax.ShapeDtypeStruct(rhs.shape, F32),
            in_specs=[hbm, hbm, hbm, hbm],
            out_specs=vm,
            scratch_shapes=scratch,
            compiler_params=pltpu.CompilerParams(
                collective_id=0, has_side_effects=True, vmem_limit_bytes=215 * 2**18
            ),
        )(rhs, diag, left_f, right_f)

    placed = (
        P("rows", "chain"),
        P(None, "rows", None),
        P(None, "rows", None),
        P(None, "rows", None),
    )
    return jax.shard_map(
        on_device, mesh=mesh, in_specs=placed, out_specs=P("rows", "chain"), check_vma=False
    )
```

time: 108 us -> 100 us (0.926)
  Pallas kernels: 107 us -> 99.2 us
    pallas_call x1, Pallas kernels: 107 us -> 99.2 us  [on_device(): pl.pallas_call(functools.partial(kernel, n_chain, levels, groups), out_sh...]
where the time goes in v3:
time: 100 us; the launch traced here: 99.9 us
  Pallas kernels  99.2 us (99%)
    pallas_call x1, Pallas kernels, on_device(): pl.pallas_call(functools.partial(kernel, n_chain, levels, groups), out_sh...  99.2 us

profile of v3, /device:TPU:1, one launch (start us, length us, event | category | flops | bytes accessed | tf_op | source)
XLA Modules:
  0.0 99.9 jit_solution(4488091412848983012)
XLA Ops:
  0.0 99.2 %shard_map.46 = f32[64,512]{1,0:T(8,128)S(1)} custom-call(f32[64,512]{1,0:T(8,128)} %rhs.1, f32[9,64,512]{2,1,0:T(8,128)} %diag.1, f32[9,64,512]{2,1,0:T(8,128)} %left_f.1, f32[9,64,512]{2,1,0:T(8,128)} %right_f.1), custom_call_target="tpu_custom_call" | custom-call | tf_op jit(solution)/shard_map/pallas_call | solution.py:397
  99.2 0.7 copy.6

commit v4 on v3

--- a/solution.py
+++ b/solution.py
@@ -13,6 +13,7 @@
 NX = 4
 NY = 4
 HALO = 8
+ORDER = (0, 2, 1, 3)
 
 
 def shift_down(v, by):
@@ -44,7 +45,7 @@
 def kernel(
     n_chain, levels, groups,
     rhs, diag, left_f, right_f, out,
-    x2, src, ybuf, g0, GN, G, fraw, f0hi, f0lo, fhi, flo, ghi, glo, prod, hs, hx, obuf, es, ex, back, zbuf, bdst, turn,
+    x2, src, ybuf, g0, GN, G2, G, fraw, f0hi, f0lo, fhi, flo, ghi, glo, prod, first_half, hs, hx, obuf, es, ex, back, zbuf, bdst, turn,
     loc_sem, fsend_sem, frecv_sem, pair_send, pair_recv, a2a_send, a2a_recv, ag_send, ag_recv, l2_recv, own_sem, known,
 ):
     C = n_chain
@@ -170,8 +171,8 @@
                     local_factor(g, f).wait()
                     remote_factor(g, f).wait_recv()
 
-    def columns(f, level, rel):
-        at = pl.multiple_of(lax.rem(x + NX - rel, NX) * R, R)
+    def columns(f, level, slot):
+        at = pl.multiple_of(lax.rem(x + NX - ORDER[slot], NX) * R, R)
         return fraw[f, level, :, :, pl.ds(at, R)].reshape(R, R)
 
     def prepare(level):
@@ -205,10 +206,12 @@
                 f0hi[f * R : (f + 1) * R, k * R : (k + 1) * R] = hi
                 f0lo[f * R : (f + 1) * R, k * R : (k + 1) * R] = (v - hi.astype(F32)).astype(BF16)
 
-    route = ((2, across), (1, right), (3, left))
+    route = ((1, across), (2, right), (3, left))
 
     def chunk(level, t, slot):
-        return GN.at[level, t, slot] if level < 2 else G.at[level - 2, t, slot]
+        if level < 2:
+            return GN.at[level, t, slot]
+        return G2.at[t, slot] if level == 2 else G.at[level - 3, t, slot]
 
     def hop(level, t, k, piece=None):
         slot, dev = route[k]
@@ -268,55 +271,85 @@
 
     prepare(2)
     for t in range(2):
-        for k in (1, 2, 0):
-            arrived(1, t, k)
-        v = jnp.concatenate([GN[1, t, rel] for rel in range(NX)], axis=1)
-        p = three_pass(padded(v), fhi[1], flo[1])[:Qh]
+        arrived(1, t, 0)
+        v = padded(jnp.concatenate((GN[1, t, 0], GN[1, t, 1]), axis=1))
+        first_half[...] = three_pass(v, fhi[1, :, : 2 * R], flo[1, :, : 2 * R])[:Qh]
+        arrived(1, t, 1)
+        arrived(1, t, 2)
+        v = padded(jnp.concatenate((GN[1, t, 2], GN[1, t, 3]), axis=1))
+        p = first_half[...] + three_pass(v, fhi[1, :, 2 * R :], flo[1, :, 2 * R :])[:Qh]
         new = p[:, :R] - shift_down(p[:, R : 2 * R], 1) - shift_up(p[:, 2 * R :], 1)
         obuf[t] = new[:Qs] if t == 0 else new[HALO:]
         for u in range(2):
-            G[0, u, 0, t * (Qs // 2) : (t + 1) * (Qs // 2), :] = obuf[t, pl.ds(u, Qs // 2, stride=2), :]
+            G2[u, 0, t * (Qs // 2) : (t + 1) * (Qs // 2), :] = obuf[t, pl.ds(u, Qs // 2, stride=2), :]
             send(2, u, t)
 
     def part(level, t, first):
-        for rel in (first, first + 1):
-            v = G[level - 2, t, rel]
+        n = Qs if level == 2 else Qs // 2
+        for slot in (first, first + 1):
+            v = chunk(level, t, slot)[...]
             hi = v.astype(BF16)
-            ghi[t, :, rel * R : (rel + 1) * R] = hi
-            glo[t, :, rel * R : (rel + 1) * R] = (v - hi.astype(F32)).astype(BF16)
+            ghi[t, :n, slot * R : (slot + 1) * R] = hi
+            glo[t, :n, slot * R : (slot + 1) * R] = (v - hi.astype(F32)).astype(BF16)
         ks = slice(first * R, (first + 2) * R)
-        a, b = ghi[t, :, ks], fhi[level, :, ks]
-        return dot_t(a, b) + dot_t(glo[t, :, ks], b) + dot_t(a, flo[level, :, ks])
+        a, b = ghi[t, :n, ks], fhi[level, :, ks]
+        return dot_t(a, b) + dot_t(glo[t, :n, ks], b) + dot_t(a, flo[level, :, ks])
 
     def finish(level, t):
+        n = Qs if level == 2 else Qs // 2
+        arrived(level, t, 0)
+        prod[t, :n] = part(level, t, 0)
         arrived(level, t, 1)
-        prod[t] = part(level, t, 0)
         arrived(level, t, 2)
-        arrived(level, t, 0)
-        p = prod[t] + part(level, t, 2)
-        by = 2 ** (level - 2)
+        p = prod[t, :n] + part(level, t, 2)
+        by = 2 ** (level - (2 if level == 2 else 3))
         return p[:, :R] - shift_down(p[:, R : 2 * R], by) - shift_up(p[:, 2 * R :], by)
 
-    for level in range(2, levels - 1):
+    prepare(3)
+    for t in range(2):
+        obuf[t] = finish(2, t)
+        for u in range(2):
+            G[0, 2 * t + u, 0] = obuf[t, pl.ds(u, Qs // 2, stride=2), :]
+            send(3, 2 * t + u)
+
+    for level in range(3, levels - 1):
         prepare(level + 1)
-        for t in range(2):
-            G[level - 1, t, 0] = finish(level, t)
-            send(level + 1, t)
-
-    for t in range(2):
-        new = finish(levels - 1, t)
-        es[t] = new
-        other = pair_copy(2 + t, es.at[t], ex.at[t])
-        other.start()
-        other.wait_recv()
-        got = turn_lanes(ex[t])
+        for w in range(4):
+            G[level - 2, w, 0] = finish(level, w)
+            send(level + 1, w)
+
+    def swapped(w):
+        t, u = w // 2, w % 2
+        pair_copy(2 + w, es.at[w], ex.at[w]).wait_recv()
+        new, got = es[w], turn_lanes(ex[w])
         both = jnp.where(low(new) == (core == 0), new, got)
-        for c in range(C):
-            back[t, c // NY, c % NY] = both[2 * c : 2 * c + 2]
-        phase(2 + t, lambda p: back.at[t, p], zbuf.at[t], z, z_others)
+        for cz in range(nz):
+            back[t, cz, :, u, :] = both[cz * NY : (cz + 1) * NY]
+        if u == 1:
+            home(t)
+
+    def home(t):
+        own = pltpu.make_async_copy(back.at[t, z, y], bdst.at[t, y, z], a2a_recv.at[2 + t])
+        for bz in range(nz // 2, -1, -1):
+            for dz in both_ways(bz) if bz else (0,):
+                for dy in range(NY):
+                    if dz or dy:
+                        pltpu.make_async_remote_copy(
+                            src_ref=back.at[t, z_of(dz), y_of(dy)], dst_ref=bdst.at[t, y, z],
+                            send_sem=a2a_send.at[2 + t], recv_sem=a2a_recv.at[2 + t],
+                            device_id=(z_of(dz) * NY + y_of(dy), rows), device_id_type=MESH,
+                        ).start()
+        own.start()
+
+    for w in range(4):
+        es[w] = finish(levels - 1, w)
+        pair_copy(2 + w, es.at[w], ex.at[w]).start()
+        if w:
+            swapped(w - 1)
+    swapped(3)
 
     for level in range(levels):
-        for t in range(2):
+        for t in range(2 if level < 3 else 4):
             sent(level, t)
     for g in range(len(groups)):
         for f in range(3):
@@ -325,13 +358,10 @@
     gone(1, ybuf.at[:, pl.ds(0, nz - 1)])
     for t in range(2):
         pair_copy(t, hs.at[t], hx.at[t]).wait_send()
-        pair_copy(2 + t, es.at[t], ex.at[t]).wait_send()
-    for t in range(2):
-        landed(2 + t, zbuf.at[t])
-        phase(4 + t, lambda p: zbuf.at[t, :, p], bdst.at[t], y, y_others)
-    for t in range(2):
-        gone(2 + t, back.at[t, pl.ds(0, nz - 1)])
-        landed(4 + t, bdst.at[t])
+    for w in range(4):
+        pair_copy(2 + w, es.at[w], ex.at[w]).wait_send()
+    for t in range(2):
+        landed(2 + t, bdst.at[t])
         for j in range(2):
             m = 2 * j + t
             for cy in range(NY):
@@ -339,7 +369,7 @@
             wide = jnp.transpose(turn[m])
             out[:, m * 2 * C : (m + 1) * 2 * C] = jnp.concatenate((wide[:dev_rows], wide[dev_rows:]), axis=1)
     for t in range(2):
-        gone(4 + t, zbuf.at[t, :, pl.ds(0, NY - 1)])
+        gone(2 + t, zbuf)
 
 
 def solution(mesh):
@@ -361,33 +391,35 @@
             pltpu.VMEM((NY, nz, n_half, R), F32),
             pltpu.VMEM((nz, NY, n_half, R), F32),
             pltpu.VMEM((2, 2, NX, Qh, R), F32),
-            pltpu.VMEM((levels - 2, 2, NX, Qs, R), F32),
+            pltpu.VMEM((2, NX, Qs, R), F32),
+            pltpu.VMEM((levels - 3, 4, NX, Qs // 2, R), F32),
             pltpu.VMEM((3, levels, 2, dev_rows, M), F32),
             pltpu.VMEM((3 * R, M // 2), BF16),
             pltpu.VMEM((3 * R, M // 2), BF16),
             pltpu.VMEM((levels, 3 * R, M), BF16),
             pltpu.VMEM((levels, 3 * R, M), BF16),
-            pltpu.VMEM((2, Qs, M), BF16),
-            pltpu.VMEM((2, Qs, M), BF16),
-            pltpu.VMEM((2, Qs, 3 * R), F32),
+            pltpu.VMEM((4, Qs, M), BF16),
+            pltpu.VMEM((4, Qs, M), BF16),
+            pltpu.VMEM((4, Qs, 3 * R), F32),
+            pltpu.VMEM((Qh, 3 * R), F32),
             pltpu.VMEM((2, Qh, R), F32),
             pltpu.VMEM((2, Qh, R), F32),
             pltpu.VMEM((2, Qs, R), F32),
-            pltpu.VMEM((2, Qs, R), F32),
-            pltpu.VMEM((2, Qs, R), F32),
+            pltpu.VMEM((4, Qs // 2, R), F32),
+            pltpu.VMEM((4, Qs // 2, R), F32),
             pltpu.VMEM((2, nz, NY, 2, R), F32),
-            pltpu.VMEM((2, nz, NY, 2, R), F32),
+            pltpu.VMEM((C - 1, 2, R), F32),
             pltpu.VMEM((2, NY, nz, 2, R), F32),
             pltpu.VMEM((n_half, C, R), F32),
             pltpu.SemaphoreType.DMA((len(groups), 3)),
             pltpu.SemaphoreType.DMA((len(groups), 3)),
             pltpu.SemaphoreType.DMA((len(groups), 3)),
+            pltpu.SemaphoreType.DMA((6,)),
+            pltpu.SemaphoreType.DMA((6,)),
             pltpu.SemaphoreType.DMA((4,)),
             pltpu.SemaphoreType.DMA((4,)),
-            pltpu.SemaphoreType.DMA((6,)),
-            pltpu.SemaphoreType.DMA((6,)),
-            pltpu.SemaphoreType.DMA((levels, 2)),
-            pltpu.SemaphoreType.DMA((levels, 2, 3)),
+            pltpu.SemaphoreType.DMA((levels, 4)),
+            pltpu.SemaphoreType.DMA((levels, 4, 3)),
             pltpu.SemaphoreType.DMA((2, 2, 3)),
             pltpu.SemaphoreType.DMA,
             pltpu.SemaphoreType.REGULAR,

time: 100 us -> 95.5 us (0.955)
  Pallas kernels: 99.2 us -> 94.7 us
    pallas_call x1, Pallas kernels: 99.2 us -> 94.7 us  [on_device(): pl.pallas_call(functools.partial(kernel, n_chain, levels, groups), out_sh...]
where the time goes in v4:
time: 95.5 us; the launch traced here: 95.3 us
  Pallas kernels  94.7 us (99%)
    pallas_call x1, Pallas kernels, on_device(): pl.pallas_call(functools.partial(kernel, n_chain, levels, groups), out_sh...  94.7 us

profile of v4, /device:TPU:1, one launch (start us, length us, event | category | flops | bytes accessed | tf_op | source)
XLA Modules:
  0.0 95.3 jit_solution(11466011285784756186)
XLA Ops:
  0.0 94.7 %shard_map.46 = f32[64,512]{1,0:T(8,128)S(1)} custom-call(f32[64,512]{1,0:T(8,128)} %rhs.1, f32[9,64,512]{2,1,0:T(8,128)} %diag.1, f32[9,64,512]{2,1,0:T(8,128)} %left_f.1, f32[9,64,512]{2,1,0:T(8,128)} %right_f.1), custom_call_target="tpu_custom_call" | custom-call | tf_op jit(solution)/shard_map/pallas_call | solution.py:429
  94.7 0.7 copy.6

commit v5 on v4

--- a/solution.py
+++ b/solution.py
@@ -46,7 +46,7 @@
     n_chain, levels, groups,
     rhs, diag, left_f, right_f, out,
     x2, src, ybuf, g0, GN, G2, G, fraw, f0hi, f0lo, fhi, flo, ghi, glo, prod, first_half, hs, hx, obuf, es, ex, back, zbuf, bdst, turn,
-    loc_sem, fsend_sem, frecv_sem, pair_send, pair_recv, a2a_send, a2a_recv, ag_send, ag_recv, l2_recv, own_sem, known,
+    loc_sem, fsend_sem, frecv_sem, pair_send, pair_recv, a2a_send, a2a_recv, ag_send, ag_recv, own_sem, known,
 ):
     C = n_chain
     nz = C // NY
@@ -96,7 +96,7 @@
     def local_factor(g, f):
         lo, hi = groups[g]
         return pltpu.make_async_copy(
-            facs[f].at[lo:hi], fraw.at[f, lo:hi, core], loc_sem.at[g, f]
+            facs[f].at[lo:hi], fraw.at[f, lo:hi, core], loc_sem.at[g]
         )
 
     own_rhs = pltpu.make_async_copy(rhs, x2, own_sem)
@@ -121,7 +121,7 @@
 
     def pair_copy(k, source, target):
         return pltpu.make_async_remote_copy(
-            src_ref=source, dst_ref=target, send_sem=pair_send.at[k], recv_sem=pair_recv.at[k],
+            src_ref=source, dst_ref=target, send_sem=pair_send.at[0 if k < 2 else 1], recv_sem=pair_recv.at[k],
             device_id=partner, device_id_type=MESH,
         )
 
@@ -129,7 +129,7 @@
         lo, hi = groups[g]
         return pltpu.make_async_remote_copy(
             src_ref=facs[f].at[lo:hi], dst_ref=fraw.at[f, lo:hi, core],
-            send_sem=fsend_sem.at[g, f], recv_sem=frecv_sem.at[g, f],
+            send_sem=fsend_sem.at[g], recv_sem=frecv_sem.at[g],
             device_id=partner, device_id_type=MESH,
         )
 
@@ -167,9 +167,9 @@
     def factors_here(level):
         for g, (lo, _) in enumerate(groups):
             if lo == level:
-                for f in range(3):
-                    local_factor(g, f).wait()
-                    remote_factor(g, f).wait_recv()
+                for sem, side in ((loc_sem, core), (frecv_sem, 1 - core)):
+                    three = fraw.at[:, lo : groups[g][1], side]
+                    pltpu.make_async_copy(three, three, sem.at[g]).wait()
 
     def columns(f, level, slot):
         at = pl.multiple_of(lax.rem(x + NX - ORDER[slot], NX) * R, R)
@@ -215,16 +215,19 @@
 
     def hop(level, t, k, piece=None):
         slot, dev = route[k]
-        source, target, recv = chunk(level, t, 0), chunk(level, t, slot), ag_recv.at[level, t, k]
+        source, target, recv = chunk(level, t, 0), chunk(level, t, slot), ag_recv.at[level % 2, t, k]
         if piece is not None:
             some = pl.ds(piece * (Qs // 2), Qs // 2)
-            source, target, recv = source.at[some], target.at[some], l2_recv.at[t, piece, k]
+            source, target, recv = source.at[some], target.at[some], ag_recv.at[0, 2 * t + piece, k]
         return pltpu.make_async_remote_copy(
-            src_ref=source, dst_ref=target, send_sem=ag_send.at[level, t], recv_sem=recv,
+            src_ref=source, dst_ref=target, send_sem=ag_send.at[level % 2, t], recv_sem=recv,
             device_id=dev, device_id_type=MESH,
         )
 
     def send(level, t, piece=None):
+        if level >= 2 and piece != 1:
+            if level >= 5 or t < 2:
+                sent(level - 2, t)
         for k in range(3):
             hop(level, t, k, piece).start()
 
@@ -237,7 +240,7 @@
 
     def sent(level, t):
         part = chunk(level, t, pl.ds(0, 3))
-        pltpu.make_async_copy(part, part, ag_send.at[level, t]).wait()
+        pltpu.make_async_copy(part, part, ag_send.at[level % 2, t]).wait()
 
     def padded(v):
         return jnp.concatenate((v, jnp.zeros((HALO, v.shape[1]), F32)), axis=0)
@@ -319,14 +322,12 @@
             send(level + 1, w)
 
     def swapped(w):
-        t, u = w // 2, w % 2
         pair_copy(2 + w, es.at[w], ex.at[w]).wait_recv()
         new, got = es[w], turn_lanes(ex[w])
         both = jnp.where(low(new) == (core == 0), new, got)
         for cz in range(nz):
-            back[t, cz, :, u, :] = both[cz * NY : (cz + 1) * NY]
-        if u == 1:
-            home(t)
+            back[w, cz, :, 0, :] = both[cz * NY : (cz + 1) * NY]
+        home(w)
 
     def home(t):
         own = pltpu.make_async_copy(back.at[t, z, y], bdst.at[t, y, z], a2a_recv.at[2 + t])
@@ -336,7 +337,7 @@
                     if dz or dy:
                         pltpu.make_async_remote_copy(
                             src_ref=back.at[t, z_of(dz), y_of(dy)], dst_ref=bdst.at[t, y, z],
-                            send_sem=a2a_send.at[2 + t], recv_sem=a2a_recv.at[2 + t],
+                            send_sem=a2a_send.at[2], recv_sem=a2a_recv.at[2 + t],
                             device_id=(z_of(dz) * NY + y_of(dy), rows), device_id_type=MESH,
                         ).start()
         own.start()
@@ -348,28 +349,24 @@
             swapped(w - 1)
     swapped(3)
 
-    for level in range(levels):
-        for t in range(2 if level < 3 else 4):
+    for level in (levels - 2, levels - 1):
+        for t in range(4):
             sent(level, t)
-    for g in range(len(groups)):
-        for f in range(3):
-            remote_factor(g, f).wait_send()
+    for g, (lo, hi) in enumerate(groups):
+        three = fraw.at[:, lo:hi, core]
+        pltpu.make_async_copy(three, three, fsend_sem.at[g]).wait()
     gone(0, src.at[:, pl.ds(0, NY - 1)])
     gone(1, ybuf.at[:, pl.ds(0, nz - 1)])
-    for t in range(2):
-        pair_copy(t, hs.at[t], hx.at[t]).wait_send()
+    for k, both in enumerate((hs, es)):
+        pltpu.make_async_copy(both, both, pair_send.at[k]).wait()
     for w in range(4):
-        pair_copy(2 + w, es.at[w], ex.at[w]).wait_send()
-    for t in range(2):
-        landed(2 + t, bdst.at[t])
-        for j in range(2):
-            m = 2 * j + t
-            for cy in range(NY):
-                turn[m, pl.ds(cy, nz, stride=NY), :] = bdst[t, cy, :, j, :]
-            wide = jnp.transpose(turn[m])
-            out[:, m * 2 * C : (m + 1) * 2 * C] = jnp.concatenate((wide[:dev_rows], wide[dev_rows:]), axis=1)
-    for t in range(2):
-        gone(2 + t, zbuf)
+        landed(2 + w, bdst.at[w])
+        m = 2 * (w % 2) + w // 2
+        for cy in range(NY):
+            turn[m, pl.ds(cy, nz, stride=NY), :] = bdst[w, cy, :, 0, :]
+        wide = jnp.transpose(turn[m])
+        out[:, m * 2 * C : (m + 1) * 2 * C] = jnp.concatenate((wide[:dev_rows], wide[dev_rows:]), axis=1)
+    gone(2, zbuf)
 
 
 def solution(mesh):
@@ -407,20 +404,19 @@
             pltpu.VMEM((2, Qs, R), F32),
             pltpu.VMEM((4, Qs // 2, R), F32),
             pltpu.VMEM((4, Qs // 2, R), F32),
-            pltpu.VMEM((2, nz, NY, 2, R), F32),
-            pltpu.VMEM((C - 1, 2, R), F32),
-            pltpu.VMEM((2, NY, nz, 2, R), F32),
+            pltpu.VMEM((4, nz, NY, 1, R), F32),
+            pltpu.VMEM((4, C - 1, 1, R), F32),
+            pltpu.VMEM((4, NY, nz, 1, R), F32),
             pltpu.VMEM((n_half, C, R), F32),
-            pltpu.SemaphoreType.DMA((len(groups), 3)),
-            pltpu.SemaphoreType.DMA((len(groups), 3)),
-            pltpu.SemaphoreType.DMA((len(groups), 3)),
+            pltpu.SemaphoreType.DMA((len(groups),)),
+            pltpu.SemaphoreType.DMA((len(groups),)),
+            pltpu.SemaphoreType.DMA((len(groups),)),
+            pltpu.SemaphoreType.DMA((2,)),
             pltpu.SemaphoreType.DMA((6,)),
+            pltpu.SemaphoreType.DMA((3,)),
             pltpu.SemaphoreType.DMA((6,)),
-            pltpu.SemaphoreType.DMA((4,)),
-            pltpu.SemaphoreType.DMA((4,)),
-            pltpu.SemaphoreType.DMA((levels, 4)),
-            pltpu.SemaphoreType.DMA((levels, 4, 3)),
-            pltpu.SemaphoreType.DMA((2, 2, 3)),
+            pltpu.SemaphoreType.DMA((2, 4)),
+            pltpu.SemaphoreType.DMA((2, 4, 3)),
             pltpu.SemaphoreType.DMA,
             pltpu.SemaphoreType.REGULAR,
         ]

time: 95.5 us -> 93.9 us (0.983)
  Pallas kernels: 94.7 us -> 93.1 us
    pallas_call x1, Pallas kernels: 94.7 us -> 93.1 us  [on_device(): pl.pallas_call(functools.partial(kernel, n_chain, levels, groups), out_sh...]
where the time goes in v5:
time: 93.9 us; the launch traced here: 93.7 us
  Pallas kernels  93.1 us (99%)
    pallas_call x1, Pallas kernels, on_device(): pl.pallas_call(functools.partial(kernel, n_chain, levels, groups), out_sh...  93.1 us

profile of v5, /device:TPU:1, one launch (start us, length us, event | category | flops | bytes accessed | tf_op | source)
XLA Modules:
  0.0 93.7 jit_solution(14613050722224193430)
XLA Ops:
  0.0 93.1 %shard_map.46 = f32[64,512]{1,0:T(8,128)S(1)} custom-call(f32[64,512]{1,0:T(8,128)} %rhs.1, f32[9,64,512]{2,1,0:T(8,128)} %diag.1, f32[9,64,512]{2,1,0:T(8,128)} %left_f.1, f32[9,64,512]{2,1,0:T(8,128)} %right_f.1), custom_call_target="tpu_custom_call" | custom-call | tf_op jit(solution)/shard_map/pallas_call | solution.py:425
  93.1 0.7 copy.6

commit v6 on v5

--- a/solution.py
+++ b/solution.py
@@ -39,13 +39,15 @@
 def three_pass(v, f_hi, f_lo):
     hi = v.astype(BF16)
     lo = (v - hi.astype(F32)).astype(BF16)
-    return dot_t(hi, f_hi) + dot_t(lo, f_hi) + dot_t(hi, f_lo)
+    n = v.shape[0]
+    p = dot_t(jnp.concatenate((hi, lo), axis=0), f_hi)
+    return p[:n] + p[n:] + dot_t(hi, f_lo)
 
 
 def kernel(
     n_chain, levels, groups,
     rhs, diag, left_f, right_f, out,
-    x2, src, ybuf, g0, GN, G2, G, fraw, f0hi, f0lo, fhi, flo, ghi, glo, prod, first_half, hs, hx, obuf, es, ex, back, zbuf, bdst, turn,
+    x2, src, ybuf, g0, GN, G2, G, fraw, f0hi, f0lo, fhi, flo, both, prod, first_half, hs, hx, obuf, es, ex, back, zbuf, bdst, turn,
     loc_sem, fsend_sem, frecv_sem, pair_send, pair_recv, a2a_send, a2a_recv, ag_send, ag_recv, own_sem, known,
 ):
     C = n_chain
@@ -288,15 +290,17 @@
             send(2, u, t)
 
     def part(level, t, first):
-        n = Qs if level == 2 else Qs // 2
+        n, base = (Qs, 4) if level == 2 else (Qs // 2, 0)
         for slot in (first, first + 1):
+            if slot == 0 and level > 2:
+                continue
             v = chunk(level, t, slot)[...]
             hi = v.astype(BF16)
-            ghi[t, :n, slot * R : (slot + 1) * R] = hi
-            glo[t, :n, slot * R : (slot + 1) * R] = (v - hi.astype(F32)).astype(BF16)
+            both[t + base, :n, slot * R : (slot + 1) * R] = hi
+            both[t + base, n : 2 * n, slot * R : (slot + 1) * R] = (v - hi.astype(F32)).astype(BF16)
         ks = slice(first * R, (first + 2) * R)
-        a, b = ghi[t, :n, ks], fhi[level, :, ks]
-        return dot_t(a, b) + dot_t(glo[t, :n, ks], b) + dot_t(a, flo[level, :, ks])
+        p = dot_t(both[t + base, : 2 * n, ks], fhi[level, :, ks])
+        return p[:n] + p[n:] + dot_t(both[t + base, :n, ks], flo[level, :, ks])
 
     def finish(level, t):
         n = Qs if level == 2 else Qs // 2
@@ -308,25 +312,30 @@
         by = 2 ** (level - (2 if level == 2 else 3))
         return p[:, :R] - shift_down(p[:, R : 2 * R], by) - shift_up(p[:, 2 * R :], by)
 
+    def own_chunk(level, w, v):
+        G[level - 3, w, 0] = v
+        send(level, w)
+        hi = v.astype(BF16)
+        both[w, : Qs // 2, :R] = hi
+        both[w, Qs // 2 : Qs, :R] = (v - hi.astype(F32)).astype(BF16)
+
     prepare(3)
     for t in range(2):
         obuf[t] = finish(2, t)
         for u in range(2):
-            G[0, 2 * t + u, 0] = obuf[t, pl.ds(u, Qs // 2, stride=2), :]
-            send(3, 2 * t + u)
+            own_chunk(3, 2 * t + u, obuf[t, pl.ds(u, Qs // 2, stride=2), :])
 
     for level in range(3, levels - 1):
         prepare(level + 1)
         for w in range(4):
-            G[level - 2, w, 0] = finish(level, w)
-            send(level + 1, w)
+            own_chunk(level + 1, w, finish(level, w))
 
     def swapped(w):
         pair_copy(2 + w, es.at[w], ex.at[w]).wait_recv()
         new, got = es[w], turn_lanes(ex[w])
-        both = jnp.where(low(new) == (core == 0), new, got)
+        packed = jnp.where(low(new) == (core == 0), new, got)
         for cz in range(nz):
-            back[w, cz, :, 0, :] = both[cz * NY : (cz + 1) * NY]
+            back[w, cz, :, 0, :] = packed[cz * NY : (cz + 1) * NY]
         home(w)
 
     def home(t):
@@ -357,8 +366,8 @@
         pltpu.make_async_copy(three, three, fsend_sem.at[g]).wait()
     gone(0, src.at[:, pl.ds(0, NY - 1)])
     gone(1, ybuf.at[:, pl.ds(0, nz - 1)])
-    for k, both in enumerate((hs, es)):
-        pltpu.make_async_copy(both, both, pair_send.at[k]).wait()
+    for k, source in enumerate((hs, es)):
+        pltpu.make_async_copy(source, source, pair_send.at[k]).wait()
     for w in range(4):
         landed(2 + w, bdst.at[w])
         m = 2 * (w % 2) + w // 2
@@ -395,8 +404,7 @@
             pltpu.VMEM((3 * R, M // 2), BF16),
             pltpu.VMEM((levels, 3 * R, M), BF16),
             pltpu.VMEM((levels, 3 * R, M), BF16),
-            pltpu.VMEM((4, Qs, M), BF16),
-            pltpu.VMEM((4, Qs, M), BF16),
+            pltpu.VMEM((6, 2 * Qs, M), BF16),
             pltpu.VMEM((4, Qs, 3 * R), F32),
             pltpu.VMEM((Qh, 3 * R), F32),
             pltpu.VMEM((2, Qh, R), F32),

time: 93.9 us -> 93.4 us (level)
  no operation moved by 1% of the time
where the time goes in v6:
time: 93.4 us; the launch traced here: 93.3 us
  Pallas kernels  92.6 us (99%)
    pallas_call x1, Pallas kernels, on_device(): pl.pallas_call(functools.partial(kernel, n_chain, levels, groups), out_sh...  92.6 us

profile of v6, /device:TPU:1, one launch (start us, length us, event | category | flops | bytes accessed | tf_op | source)
XLA Modules:
  0.0 93.3 jit_solution(17598388794952132648)
XLA Ops:
  0.0 92.6 %shard_map.46 = f32[64,512]{1,0:T(8,128)S(1)} custom-call(f32[64,512]{1,0:T(8,128)} %rhs.1, f32[9,64,512]{2,1,0:T(8,128)} %diag.1, f32[9,64,512]{2,1,0:T(8,128)} %left_f.1, f32[9,64,512]{2,1,0:T(8,128)} %right_f.1), custom_call_target="tpu_custom_call" | custom-call | tf_op jit(solution)/shard_map/pallas_call | solution.py:433
  92.6 0.7 copy.6

commit v7 on v6

--- a/solution.py
+++ b/solution.py
@@ -14,22 +14,6 @@
 NY = 4
 HALO = 8
 ORDER = (0, 2, 1, 3)
-
-
-def shift_down(v, by):
-    n, w = v.shape
-    if by % 8 == 0:
-        return jnp.concatenate((jnp.zeros((by, w), v.dtype), v[: n - by]), axis=0)
-    rows = lax.broadcasted_iota(jnp.int32, v.shape, 0)
-    return jnp.where(rows < by, 0.0, pltpu.roll(v, by, 0))
-
-
-def shift_up(v, by):
-    n, w = v.shape
-    if by % 8 == 0:
-        return jnp.concatenate((v[by:], jnp.zeros((by, w), v.dtype)), axis=0)
-    rows = lax.broadcasted_iota(jnp.int32, v.shape, 0)
-    return jnp.where(rows >= n - by, 0.0, pltpu.roll(v, n - by, 0))
 
 
 def dot_t(a, b):
@@ -57,7 +41,7 @@
     n_half = src.shape[2]
     Q = C * n_half
     Qs = Q // 2
-    Qh = Qs + HALO
+    Qh = Qs + 2 * HALO
     chain = lax.axis_index("chain")
     rows = lax.axis_index("rows")
     core = lax.rem(rows, 2)
@@ -152,10 +136,6 @@
         pltpu.make_async_copy(part, part, a2a_send.at[k]).wait()
 
     y_others = [(y_of(b), y_dev(b)) for b in range(1, NY)]
-    z_others = []
-    for b in range(nz // 2, 0, -1):
-        for by in both_ways(b):
-            z_others.append((z_of(by), z_dev(by)))
 
     phase(0, lambda p: src.at[:, p], ybuf, y, y_others)
     for g in range(len(groups)):
@@ -164,7 +144,24 @@
     landed(0, ybuf)
     if far:
         pl.semaphore_wait(known, 2)
-    phase(1, lambda p: ybuf.at[:, p], g0, z, z_others)
+    zsh = nz // 4
+    near_n = min(nz, nz // 2 + 2)
+    offset = lax.rem(z - zsh + nz, nz) * (NY * n_half)
+
+    def slot_of(by):
+        return (zsh + 1 - by) % nz
+
+    def part_of(by):
+        return 1 if slot_of(by) < near_n else 2
+
+    here = pltpu.make_async_copy(ybuf.at[:, z], g0.at[slot_of(0)], a2a_recv.at[1])
+    for by in sorted((b for n in range(1, nz // 2 + 1) for b in both_ways(n)), key=part_of):
+        pltpu.make_async_remote_copy(
+            src_ref=ybuf.at[:, z_of(by)], dst_ref=g0.at[slot_of(by)],
+            send_sem=a2a_send.at[1], recv_sem=a2a_recv.at[part_of(by)],
+            device_id=z_dev(by), device_id_type=MESH,
+        ).start()
+    here.start()
 
     def factors_here(level):
         for g, (lo, _) in enumerate(groups):
@@ -244,16 +241,32 @@
         part = chunk(level, t, pl.ds(0, 3))
         pltpu.make_async_copy(part, part, ag_send.at[level % 2, t]).wait()
 
-    def padded(v):
-        return jnp.concatenate((v, jnp.zeros((HALO, v.shape[1]), F32)), axis=0)
+    def place(v, start, count):
+        at = lax.broadcasted_iota(jnp.int32, v.shape, 0) + start
+        return jnp.where(at >= count, at - count, at)
+
+    def rolled(v, by):
+        n = v.shape[0]
+        if by % 8 or not by < n:
+            return pltpu.roll(v, by % n, 0)
+        return jnp.concatenate((v[n - by :], v[: n - by]), axis=0)
+
+    def below(v, by, start, count):
+        return jnp.where(place(v, start, count) < by, 0.0, rolled(v, by))
+
+    def above(v, by, start, count):
+        return jnp.where(place(v, start, count) >= count - by, 0.0, rolled(v, v.shape[0] - by))
 
     prepare_first()
-    landed(1, g0)
-    first = (0, (Qs - HALO) // n_half)
+    begins = [lax.rem(offset + t * Qs + Q - HALO, Q) for t in range(2)]
     for t in range(2):
+        if t == 0:
+            landed(1, g0.at[pl.ds(0, near_n)])
+        elif near_n < nz:
+            landed(2, g0.at[pl.ds(near_n, nz - near_n)])
         for i in range(Qh // n_half):
-            c = first[t] + i
-            GN[0, t, 0, i * n_half : (i + 1) * n_half, :] = g0[c // NY, c % NY]
+            c = (t * Qs - HALO) // n_half + i
+            GN[0, t, 0, i * n_half : (i + 1) * n_half, :] = g0[(c // NY + 1) % nz, c % NY]
         send(0, t)
     prepare(1)
     for t in range(2):
@@ -261,30 +274,38 @@
             arrived(0, t, k)
         a = [GN[0, t, rel] for rel in range(NX)]
         ev = jnp.concatenate((firsts(a[0], a[1]), firsts(a[2], a[3])), axis=1)
-        pe = three_pass(padded(ev), f0hi[...], f0lo[...])[:Qh]
+        pe = three_pass(ev, f0hi[...], f0lo[...])
         od = jnp.concatenate((seconds(a[0], a[1]), seconds(a[2], a[3])), axis=1)
-        po = three_pass(padded(od), f0hi[...], f0lo[...])[:Qh]
-        to_even = pe[:, :R] - shift_down(po[:, R : 2 * R], 1) - po[:, 2 * R :]
-        to_odd = po[:, :R] - pe[:, R : 2 * R] - shift_up(pe[:, 2 * R :], 1)
+        po = three_pass(od, f0hi[...], f0lo[...])
+        to_even = pe[:, :R] - below(po[:, R : 2 * R], 1, begins[t], Q) - po[:, 2 * R :]
+        to_odd = po[:, :R] - pe[:, R : 2 * R] - above(pe[:, 2 * R :], 1, begins[t], Q)
         hs[t] = jnp.where(core == 0, to_odd, to_even)
-        other = pair_copy(t, hs.at[t], hx.at[t])
-        other.start()
-        mine = jnp.where(core == 0, to_even, to_odd)
-        other.wait_recv()
-        GN[1, t, 0] = mine + hx[t]
-        send(1, t)
+        pair_copy(t, hs.at[t], hx.at[t]).start()
+        GN[1, t, 0] = jnp.where(core == 0, to_even, to_odd)
+
+        def joined(t=t):
+            pair_copy(t, hs.at[t], hx.at[t]).wait_recv()
+            GN[1, t, 0] = GN[1, t, 0] + hx[t]
+            send(1, t)
+
+        if t == 0:
+            waiting = joined
+            pl.when(core == 0)(joined)
+        else:
+            pl.when(core == 1)(waiting)
+            joined()
 
     prepare(2)
     for t in range(2):
         arrived(1, t, 0)
-        v = padded(jnp.concatenate((GN[1, t, 0], GN[1, t, 1]), axis=1))
-        first_half[...] = three_pass(v, fhi[1, :, : 2 * R], flo[1, :, : 2 * R])[:Qh]
+        v = jnp.concatenate((GN[1, t, 0], GN[1, t, 1]), axis=1)
+        first_half[...] = three_pass(v, fhi[1, :, : 2 * R], flo[1, :, : 2 * R])
         arrived(1, t, 1)
         arrived(1, t, 2)
-        v = padded(jnp.concatenate((GN[1, t, 2], GN[1, t, 3]), axis=1))
-        p = first_half[...] + three_pass(v, fhi[1, :, 2 * R :], flo[1, :, 2 * R :])[:Qh]
-        new = p[:, :R] - shift_down(p[:, R : 2 * R], 1) - shift_up(p[:, 2 * R :], 1)
-        obuf[t] = new[:Qs] if t == 0 else new[HALO:]
+        v = jnp.concatenate((GN[1, t, 2], GN[1, t, 3]), axis=1)
+        p = first_half[...] + three_pass(v, fhi[1, :, 2 * R :], flo[1, :, 2 * R :])
+        new = p[:, :R] - below(p[:, R : 2 * R], 1, begins[t], Q) - above(p[:, 2 * R :], 1, begins[t], Q)
+        obuf[t] = new[HALO : HALO + Qs]
         for u in range(2):
             G2[u, 0, t * (Qs // 2) : (t + 1) * (Qs // 2), :] = obuf[t, pl.ds(u, Qs // 2, stride=2), :]
             send(2, u, t)
@@ -310,7 +331,8 @@
         arrived(level, t, 2)
         p = prod[t, :n] + part(level, t, 2)
         by = 2 ** (level - (2 if level == 2 else 3))
-        return p[:, :R] - shift_down(p[:, R : 2 * R], by) - shift_up(p[:, 2 * R :], by)
+        start = offset // (Q // n)
+        return p[:, :R] - below(p[:, R : 2 * R], by, start, n) - above(p[:, 2 * R :], by, start, n)
 
     def own_chunk(level, w, v):
         G[level - 3, w, 0] = v
@@ -339,14 +361,14 @@
         home(w)
 
     def home(t):
-        own = pltpu.make_async_copy(back.at[t, z, y], bdst.at[t, y, z], a2a_recv.at[2 + t])
+        own = pltpu.make_async_copy(back.at[t, zsh, y], bdst.at[t, y, z], a2a_recv.at[3 + t])
         for bz in range(nz // 2, -1, -1):
             for dz in both_ways(bz) if bz else (0,):
                 for dy in range(NY):
                     if dz or dy:
                         pltpu.make_async_remote_copy(
-                            src_ref=back.at[t, z_of(dz), y_of(dy)], dst_ref=bdst.at[t, y, z],
-                            send_sem=a2a_send.at[2], recv_sem=a2a_recv.at[2 + t],
+                            src_ref=back.at[t, (zsh + dz) % nz, y_of(dy)], dst_ref=bdst.at[t, y, z],
+                            send_sem=a2a_send.at[2], recv_sem=a2a_recv.at[3 + t],
                             device_id=(z_of(dz) * NY + y_of(dy), rows), device_id_type=MESH,
                         ).start()
         own.start()
@@ -369,7 +391,7 @@
     for k, source in enumerate((hs, es)):
         pltpu.make_async_copy(source, source, pair_send.at[k]).wait()
     for w in range(4):
-        landed(2 + w, bdst.at[w])
+        landed(3 + w, bdst.at[w])
         m = 2 * (w % 2) + w // 2
         for cy in range(NY):
             turn[m, pl.ds(cy, nz, stride=NY), :] = bdst[w, cy, :, 0, :]
@@ -389,7 +411,7 @@
         nz = C // NY
         Q = C * n_half
         Qs = Q // 2
-        Qh = Qs + HALO
+        Qh = Qs + 2 * HALO
         groups = ((0, 1), (1, 3), (3, levels))
         scratch = [
             pltpu.VMEM(rhs.shape, F32),
@@ -422,7 +444,7 @@
             pltpu.SemaphoreType.DMA((2,)),
             pltpu.SemaphoreType.DMA((6,)),
             pltpu.SemaphoreType.DMA((3,)),
-            pltpu.SemaphoreType.DMA((6,)),
+            pltpu.SemaphoreType.DMA((7,)),
             pltpu.SemaphoreType.DMA((2, 4)),
             pltpu.SemaphoreType.DMA((2, 4, 3)),
             pltpu.SemaphoreType.DMA,

time: 93.4 us -> 92.9 us (level)
  no operation moved by 1% of the time
where the time goes in v7:
time: 92.9 us; the launch traced here: 92.8 us
  Pallas kernels  92.2 us (99%)
    pallas_call x1, Pallas kernels, on_device(): pl.pallas_call(functools.partial(kernel, n_chain, levels, groups), out_sh...  92.2 us

profile of v7, /device:TPU:1, one launch (start us, length us, event | category | flops | bytes accessed | tf_op | source)
XLA Modules:
  0.0 92.8 jit_solution(15076635993267531358)
XLA Ops:
  0.0 92.2 %shard_map.46 = f32[64,512]{1,0:T(8,128)S(1)} custom-call(f32[64,512]{1,0:T(8,128)} %rhs.1, f32[9,64,512]{2,1,0:T(8,128)} %diag.1, f32[9,64,512]{2,1,0:T(8,128)} %left_f.1, f32[9,64,512]{2,1,0:T(8,128)} %right_f.1), custom_call_target="tpu_custom_call" | custom-call | tf_op jit(solution)/shard_map/pallas_call | solution.py:455
  92.2 0.7 copy.6
